TPU v7x, 256 devices: a whole 4x4x8 slice. The times are simulated.
256 devices in a mesh: corpus: 32 (over z_lo, x, core), query: 8 (over z_hi, y).
Axes of the slice: x: 4, y: 4, z: 8 (z_hi: 2, z_lo: 4; z = z_hi * 4 + z_lo), core: 2. Of those that a mesh axis runs over, the one named last changes fastest.
Arguments:
- inputs: bfloat16 [131072, 4096], P(('corpus', 'query'))
- cotangents: bfloat16 [131072, 4096], P(('corpus', 'query')), may hold values from -6 to 6
- sketch_maps: bfloat16 [4096, 128], replicated, may hold values from -0.09375 to 0.09375
- lengths: int32 [1024], P(('corpus', 'query')), may hold values from 1 to 128, 81920 in all
- queries: bfloat16 [2048, 4096], P(('query', 'corpus')), may hold values from -0.09375 to 0.09375
Outputs:
- scores: float32 [131072, 2048], P('corpus', 'query')
Inputs may be any that keep to these rules, and one draw needn't show every extreme that they name: `lengths`: each training sequence has at least one live token; some sequence has 128.
All inputs are finite; a program needn't handle non-finite values. No bound on the sum of `lengths` on one device may be relied on, other than what follows from the above.
Results may differ from a plain program's by a relative error of at most 0.005.
Values may be sent and summed in bfloat16 or wider, within the bound.
No kernel may reach another device: no remote copies, remote signals or barrier semaphores. Data moves between devices by JAX's collectives and lax.ppermute only.
A program may use at most 128 MiB of HBM per device.

v0:
```python
import jax
import jax.numpy as jnp
from jax import lax
from jax.sharding import PartitionSpec as P


def damped_inverse(moment):
    size = moment.shape[0]
    identity = jnp.eye(size, dtype=jnp.float32)
    damped = moment + 0.1 * jnp.trace(moment) / size * identity
    factor = jnp.linalg.cholesky(damped)
    return jax.scipy.linalg.cho_solve((factor, True), identity)


def condition(query_block, inverse_out, inverse_in):
    number = query_block.shape[0]
    size = inverse_in.shape[0]
    matrices = query_block.astype(jnp.float32).reshape(number, size, size)
    left = jnp.einsum("ik,qkj->qij", inverse_out, matrices, precision=lax.Precision.HIGHEST)
    both = jnp.einsum("qik,kj->qij", left, inverse_in, precision=lax.Precision.HIGHEST)
    return both.reshape(number, size * size).astype(jnp.bfloat16)


def shards(inputs, cotangents, sketch_maps, lengths, queries):
    sketch_rank = sketch_maps.shape[1] // 2
    slot_length = inputs.shape[0] // lengths.shape[0]
    live_mask = (
        (jnp.arange(slot_length, dtype=jnp.int32)[None, :] < lengths[:, None])
        .reshape(-1)
        .astype(jnp.float32)
    )
    side_in = (
        jnp.dot(inputs, sketch_maps[:, :sketch_rank], preferred_element_type=jnp.float32)
        * live_mask[:, None]
    )
    side_out = (
        jnp.dot(cotangents, sketch_maps[:, sketch_rank:], preferred_element_type=jnp.float32)
        * live_mask[:, None]
    )
    local_in = jnp.dot(side_in.T, side_in, precision=lax.Precision.HIGHEST)
    local_out = jnp.dot(side_out.T, side_out, precision=lax.Precision.HIGHEST)
    summed_in, summed_out, counted = lax.psum(
        (local_in, local_out, jnp.sum(live_mask)), ("corpus", "query")
    )
    inverse_in = damped_inverse(summed_in / counted)
    inverse_out = damped_inverse(summed_out / counted)
    prepared = condition(queries, inverse_out, inverse_in)
    conditioned = lax.all_gather(prepared, "corpus", axis=0, tiled=True)
    piece_in, piece_out = lax.all_gather((side_in, side_out), "query", axis=0, tiled=True)
    piece_rows = piece_in.shape[0]
    sketch = (
        (piece_out[:, :, None] * piece_in[:, None, :])
        .reshape(piece_rows, sketch_rank * sketch_rank)
        .astype(jnp.bfloat16)
    )
    return lax.dot_general(
        sketch, conditioned, (((1,), (1,)), ((), ())), preferred_element_type=jnp.float32
    )


def solution(mesh):
    placed = (
        P(("corpus", "query"), None),
        P(("corpus", "query"), None),
        P(),
        P(("corpus", "query")),
        P(("query", "corpus"), None),
    )
    return jax.shard_map(
        shards, mesh=mesh, in_specs=placed, out_specs=P("corpus", "query"), check_vma=False
    )
```

profile of v0, /device:TPU:24, one launch (start us, length us, event | category | flops | bytes accessed | tf_op | source)
XLA Modules:
  0.0 219.6 jit_solution(693176517676573688)
XLA Ops:
  6.5 0.8 convert_bitcast_fusion
  7.4 4.5 %convolution_multiply_fusion = f32[512,64]{0,1:T(8,128)} fusion(bf16[512,4096]{1,0:T(8,128)(2,1)} %param.8, bf16[4096,128]{1,0:T(8,128)(2,1)} %param.10, f32[512]{0:T(512)S(1)} %convert_bitcast_fusion), kind=kOutput, calls=%fused_computation.3 | convolution fusion | flops 268468224 | bytes 5376000 | tf_op jit(solution)/shard_map/dot_general | solution.py:33
  11.9 0.0 all-gather.4.cloned.1.call-start
  12.0 4.6 %convolution_multiply_fusion.1 = f32[512,64]{0,1:T(8,128)} fusion(bf16[512,4096]{1,0:T(8,128)(2,1)} %param.9, bf16[4096,128]{1,0:T(8,128)(2,1)S(1)} %copy-done, f32[512]{0:T(512)S(1)} %convert_bitcast_fusion), kind=kOutput, calls=%fused_computation.4 | convolution fusion | flops 268468224 | bytes 5376000 | tf_op jit(solution)/shard_map/dot_general | solution.py:37
  16.7 0.7 convert_reduce_fusion
  17.4 0.3 fusion.15
  17.7 1.2 fusion.14
  18.9 87.2 %all-reduce = (f32[64,64]{0,1:T(8,128)S(1)}, f32[]{:T(128)}, f32[64,64]{0,1:T(8,128)S(1)}) all-reduce(f32[64,64]{0,1:T(8,128)S(1)} %fusion.14, f32[]{:T(128)} %convert_reduce_fusion, f32[64,64]{0,1:T(8,128)S(1)} %fusion.15), channel_id=1, replica_groups=mesh['corpus'=32,'query'=8] {'corpus','query'}, use_global_device_ids=true, to_apply=%region_0.0 | all-reduce | flops 8193 | bytes 65544 | tf_op jit(solution)/shard_map/psum | solution.py:42
  106.1 1.2 select_reduce_fusion.2
  107.3 1.3 select_reduce_fusion.3
  109.9 0.6 select_add_fusion
  110.5 0.1 copy.19
  110.6 5.8 %cholesky.55 = f32[64,64]{1,0:T(8,128)S(1)} custom-call(f32[64,64]{1,0:T(8,128)S(1)} %fusion.10), custom_call_target="Cholesky" | custom-call | tf_op jit(solution)/shard_map/jit(cholesky)/cholesky | solution.py:11
  116.5 0.6 compare_reduce_fusion
  117.1 0.6 fusion.7
  117.7 4.9 %custom-call.9 = f32[1,64,64]{1,2,0:T(8,128)S(1)} custom-call(f32[1,64,64]{2,1,0:T(8,128)S(1)} %fusion.7), custom_call_target="InvertDiagBlocksLowerTriangular" | custom-call | tf_op jit(solution)/shard_map/jit(_cho_solve)/triangular_solve | solution.py:12
  122.6 0.1 copy.17
  122.7 5.8 %cholesky.44 = f32[64,64]{1,0:T(8,128)S(1)} custom-call(f32[64,64]{1,0:T(8,128)S(1)} %fusion.13), custom_call_target="Cholesky" | custom-call | tf_op jit(solution)/shard_map/jit(cholesky)/cholesky | solution.py:11
  128.6 0.6 compare_reduce_fusion.1
  129.2 0.6 fusion.6
  129.8 4.9 %custom-call.8 = f32[1,64,64]{1,2,0:T(8,128)S(1)} custom-call(f32[1,64,64]{2,1,0:T(8,128)S(1)} %fusion.6), custom_call_target="InvertDiagBlocksLowerTriangular" | custom-call | tf_op jit(solution)/shard_map/jit(_cho_solve)/triangular_solve | solution.py:12
  134.7 0.2 reshape.39
  134.9 0.2 fusion.2
  135.1 0.2 convolution_bitcast_fusion.1
  135.3 0.2 fusion.4
  135.6 0.2 convolution_bitcast_fusion.2
  135.7 0.3 convolution_bitcast_fusion
  136.0 0.4 convolution_convert_fusion
  136.3 0.8 convert_element_type.39
  137.2 13.8 %multiply_convert_fusion = bf16[4096,64,64]{0,2,1:T(8,128)(2,1)} fusion(f32[4096,64]{0,1:T(8,128)} %all-gather.6.cloned.1.call-done, f32[4096,64]{0,1:T(8,128)} %all-gather.4.cloned.1.call-done), kind=kLoop, calls=%fused_computation | loop fusion | flops 33554432 | bytes 35651584 | tf_op jit(solution)/shard_map/convert_element_type | solution.py:54
  151.1 44.3 %all-gather.8.cloned.1.call-done = bf16[256,4096]{1,0:T(8,128)(2,1)} async-done(((bf16[8,4096]{1,0:T(8,128)(2,1)}), bf16[256,4096]{1,0:T(8,128)(2,1)}) %all-gather.8.cloned.1.call-update) | async-done | bytes 2097168 | tf_op jit(solution)/shard_map/all_gather | solution.py:48
  195.4 17.6 %fusion.16 = f32[4096,256]{1,0:T(8,128)} fusion(bf16[4096,4096]{0,1:T(8,128)(2,1)} %bitcast.45, bf16[256,4096]{1,0:T(8,128)(2,1)} %all-gather.8.cloned.1.call-done), kind=kOutput, calls=%fused_computation.43 | convolution fusion | flops 8589934592 | bytes 39845888 | tf_op jit(solution)/shard_map/dot_general | solution.py:56
  (19 shorter events, 0.2 us)
Async XLA Ops:
  6.5 5.5 %copy-start = (bf16[4096,128]{1,0:T(8,128)(2,1)S(1)}, bf16[4096,128]{1,0:T(8,128)(2,1)}, u32[]{:S(2)}) copy-start(bf16[4096,128]{1,0:T(8,128)(2,1)} %param.10) | copy-start | bytes 3145732
  6.5 130.7 %all-gather.6.cloned.1.call-start = ((), (), s32[]{:S(2)}) async-start(), calls=%async_computation.1 | async-start | bytes 1179648 | tf_op jit(solution)/shard_map/all_gather | solution.py:49
  11.9 4.8 %copy-start.3 = (s32[4]{0:T(128)S(1)}, s32[4]{0:T(128)}, u32[]{:S(2)}) copy-start(s32[4]{0:T(128)} %param.11) | copy-start | bytes 52
  11.9 5.5 %copy-start.1 = (f32[512,64]{0,1:T(8,128)S(1)}, f32[512,64]{0,1:T(8,128)}, u32[]{:S(2)}) copy-start(f32[512,64]{0,1:T(8,128)} %convolution_multiply_fusion) | copy-start | bytes 393220
  11.9 122.8 %copy-start.2 = (bf16[8,4096]{1,0:T(8,128)(2,1)S(1)}, bf16[8,4096]{1,0:T(8,128)(2,1)}, u32[]{:S(2)}) copy-start(bf16[8,4096]{1,0:T(8,128)(2,1)} %param.12) | copy-start | bytes 196612
  11.9 125.3 %all-gather.4.cloned.1.call-start = ((), (), s32[]{:S(2)}) async-start(), calls=%async_computation | async-start | bytes 1179648 | tf_op jit(solution)/shard_map/all_gather | solution.py:49
  16.6 178.8 %all-gather.8.cloned.1.call-start = ((), (), s32[]{:S(2)}) async-start(), calls=%async_computation.2 | async-start | bytes 2162688 | tf_op jit(solution)/shard_map/all_gather | solution.py:48
Sparse Core Ops, SparseCore 0:
  12.0 64.6 all-gather.5
  79.4 57.5 all-gather.3
  138.8 56.5 all-gather.7
where the time goes:
time: 221 us; the launch traced here: 220 us
  blocking collectives  87.2 us (39%)
  waiting for transfers between devices  44.4 us (20%)
  other arithmetic  42.5 us (19%)
  matrix products  29.6 us (13%)
  between operations  14.5 us (7%)
    psum x1, blocking collectives, shards(): lax.psum((local_in, local_out, jnp.sum(live_mask)), ('corpus', 'query'))  87.2 us
    all_gather x1, waiting for transfers between devices, shards(): conditioned = lax.all_gather(prepared, 'corpus', axis=0, tiled=True)  44.3 us
    dot_general x1, matrix products, shards(): lax.dot_general(sketch, conditioned, (((1,), (1,)), ((), ())), preferred_...  17.6 us
    convert_element_type x1, other arithmetic, shards(): sketch = (piece_out[:, :, None] * piece_in[:, None, :]).reshape(piece_row...  13.8 us
    another operation x6, other arithmetic, damped_inverse(): factor = jnp.linalg.cholesky(damped)  13 us
    another operation x4, other arithmetic, damped_inverse(): return jax.scipy.linalg.cho_solve((factor, True), identity)  10.9 us
    dot_general x1, matrix products, shards(): jnp.dot(cotangents, sketch_maps[:, sketch_rank:], preferred_element_type=...  4.59 us
    dot_general x1, matrix products, shards(): jnp.dot(inputs, sketch_maps[:, :sketch_rank], preferred_element_type=jnp....  4.54 us
  transfers between devices with their start and end apart: 3, of which 1 were waited for; matrix products, arithmetic and copies ran while one was open for 23% of the time, Pallas kernels for 0%

commit v1 on v0

v1 whole, which is shorter than its diff:
```python
import functools

import jax
import jax.numpy as jnp
from jax import lax
from jax.experimental import pallas as pl
from jax.experimental.pallas import tpu as pltpu
from jax.sharding import PartitionSpec as P

F32 = jnp.float32
BF16 = jnp.bfloat16
BOTH = ("corpus", "query")
NT = (((1,), (1,)), ((), ()))
TN = (((0,), (0,)), ((), ()))
MIB = 1 << 20


def exchange(array, corpus_bits, query_bits):
    pairs = [
        (c * 8 + q, (c ^ corpus_bits) * 8 + (q ^ query_bits))
        for c in range(32)
        for q in range(8)
    ]
    return lax.ppermute(array, BOTH, pairs)


def along_z(array, partner):
    pairs = []
    for c in range(32):
        for q in range(8):
            z = partner[(q >> 2) * 4 + (c >> 3)]
            pairs.append((c * 8 + q, ((z & 3) * 8 + (c & 7)) * 8 + (z >> 2) * 4 + (q & 3)))
    return lax.ppermute(array, BOTH, pairs)


def sum_over_all(part):
    part = part + exchange(part, 1, 0)
    part = part + exchange(part, 2, 0)
    part = part + exchange(part, 6, 0)
    part = part + exchange(part, 0, 1)
    part = part + exchange(part, 0, 3)
    part = part + along_z(part, (1, 0, 3, 2, 5, 4, 7, 6))
    part = part + along_z(part, (7, 2, 1, 4, 3, 6, 5, 0))
    return part + along_z(part, (3, 6, 5, 0, 7, 2, 1, 4))


def sides_kernel(lengths_ref, inputs_ref, cotangents_ref, maps_ref, sides_ref, sums_ref):
    step = pl.program_id(0)
    rank = maps_ref.shape[1] // 2
    rows = inputs_ref.shape[0]
    maps = maps_ref[...]
    of_in = jnp.dot(inputs_ref[...], maps, preferred_element_type=F32)
    of_out = jnp.dot(cotangents_ref[...], maps, preferred_element_type=F32)
    lane = lax.broadcasted_iota(jnp.int32, of_in.shape, 1)
    row = lax.broadcasted_iota(jnp.int32, of_in.shape, 0)
    length = lengths_ref[step]
    sides = jnp.where(row < length, jnp.where(lane < rank, of_in, of_out), 0.0)
    sides_ref[...] = sides.astype(BF16)
    gram = lax.dot_general(sides, sides, TN, precision=lax.Precision.HIGHEST, preferred_element_type=F32)
    half = lax.broadcasted_iota(jnp.int32, (rank, 2 * rank), 1) < rank

    @pl.when(step == 0)
    def _():
        sums_ref[...] = jnp.zeros_like(sums_ref)

    sums_ref[:rank, :] += jnp.where(half, gram[:rank], gram[rank:])
    sums_ref[rank:, :] += jnp.full((8, 2 * rank), 1.0, F32) * length.astype(F32)


def sides_and_sums(inputs, cotangents, sketch_maps, lengths):
    rows, width = inputs.shape
    sequences = lengths.shape[0]
    slots = rows // sequences
    both = sketch_maps.shape[1]
    return pl.pallas_call(
        sides_kernel,
        grid_spec=pltpu.PrefetchScalarGridSpec(
            num_scalar_prefetch=1,
            grid=(sequences,),
            in_specs=[
                pl.BlockSpec((slots, width), lambda i, n: (i, 0)),
                pl.BlockSpec((slots, width), lambda i, n: (i, 0)),
                pl.BlockSpec((width, both), lambda i, n: (0, 0)),
            ],
            out_specs=[
                pl.BlockSpec((slots, both), lambda i, n: (i, 0)),
                pl.BlockSpec((both // 2 + 8, both), lambda i, n: (0, 0)),
            ],
        ),
        out_shape=[
            jax.ShapeDtypeStruct((rows, both), BF16),
            jax.ShapeDtypeStruct((both // 2 + 8, both), F32),
        ],
        compiler_params=pltpu.CompilerParams(vmem_limit_bytes=24 * MIB),
        cost_estimate=pl.CostEstimate(
            flops=4 * rows * width * both, bytes_accessed=4 * rows * width, transcendentals=0
        ),
    )(lengths, inputs, cotangents, sketch_maps)


def damped_inverses(sums):
    rank = sums.shape[0] - 8
    shape = (rank, 2 * rank)
    row = lax.broadcasted_iota(jnp.int32, shape, 0)
    lane = lax.broadcasted_iota(jnp.int32, shape, 1)
    left = lane < rank
    column = jnp.where(left, lane, lane - rank)
    moment = sums[:rank] / sums[rank : rank + 1]
    diagonal = jnp.where(row == column, moment, 0.0)
    trace_in = jnp.sum(jnp.where(left, diagonal, 0.0))
    trace_out = jnp.sum(jnp.where(left, 0.0, diagonal))
    damping = 0.1 / rank * jnp.where(left, trace_in, trace_out)
    work = moment + jnp.where(row == column, damping, 0.0)
    for k in range(rank):
        pivot_column = jnp.where(left, work[:, k : k + 1], work[:, rank + k : rank + k + 1])
        at_column = column == k
        inverse = 1.0 / pivot_column[k : k + 1]
        pivot_row = jnp.where(at_column[:1], 1.0, work[k : k + 1]) * inverse
        swept = jnp.where(at_column, 0.0, work) - pivot_column * pivot_row
        work = jnp.where(row == k, pivot_row, swept)
    return work


def scores_kernel(place_ref, sums_ref, near_ref, far_ref, *rest, tile):
    *parts, out_ref, held, blocks, first, second, lhs, turned, moved, sem = rest
    step, steps = pl.program_id(0), pl.num_programs(0)
    rank = sums_ref.shape[0] - 8
    near = near_ref.shape[0]
    part = parts[0].shape[0]

    def build(index, into):
        sides = blocks[pl.ds(pl.multiple_of(index * tile, tile), tile), :]
        turned[...] = lax.dot_general(lhs[0], sides, NT, preferred_element_type=F32) + lax.dot_general(
            lhs[1], sides, NT, preferred_element_type=F32
        )
        of_in = turned[:rank, :]
        for i in range(rank):
            into[i * rank : (i + 1) * rank, :] = (turned[rank + i : rank + i + 1, :] * of_in).astype(BF16)

    def score(sketch, half):
        product = jnp.dot(held[...], sketch[...], preferred_element_type=F32)
        for slot in range(product.shape[0] // 8):
            difference = (slot & 3) * 8 + ((slot >> 2) & 3) * 2 + (slot >> 4)
            target = pl.multiple_of((place_ref[0] ^ difference) * 8, 8)
            moved[pl.ds(target, 8), :] = product[slot * 8 : (slot + 1) * 8, :]
        out_ref[half * tile : (half + 1) * tile, :] = moved[...].T

    @pl.when(step == 0)
    def _():
        copies = [
            pltpu.make_async_copy(near_ref, held.at[pl.ds(0, near), :], sem.at[0]),
            pltpu.make_async_copy(far_ref, held.at[pl.ds(near, near), :], sem.at[1]),
        ]
        for i, ref in enumerate(parts):
            copies.append(pltpu.make_async_copy(ref, blocks.at[pl.ds(i * part, part), :], sem.at[2 + i]))
        for copy in copies:
            copy.start()
        inverses = damped_inverses(sums_ref[...])
        left = lax.broadcasted_iota(jnp.int32, inverses.shape, 1) < rank
        whole = jnp.concatenate([jnp.where(left, inverses, 0.0), jnp.where(left, 0.0, inverses)])
        high = whole.astype(BF16)
        lhs[0] = high
        lhs[1] = (whole - high.astype(F32)).astype(BF16)
        for copy in copies:
            copy.wait()
        build(0, first)

    score(first, 0)
    build(2 * step + 1, second)
    score(second, 1)
    build(jnp.minimum(2 * step + 2, 2 * steps - 2), first)


def scores_of(place, sums, near, far, parts, tile=256):
    both = sums.shape[1]
    number, entries = 2 * near.shape[0], near.shape[1]
    rows = sum(part.shape[0] for part in parts)
    steps = rows // (2 * tile)
    anywhere = pl.BlockSpec(memory_space=pl.ANY)
    return pl.pallas_call(
        functools.partial(scores_kernel, tile=tile),
        grid_spec=pltpu.PrefetchScalarGridSpec(
            num_scalar_prefetch=1,
            grid=(steps,),
            in_specs=[pl.BlockSpec(sums.shape, lambda i, p: (0, 0))] + [anywhere] * (2 + len(parts)),
            out_specs=pl.BlockSpec(
                (2 * tile, number), lambda i, p: (p[1] ^ ((i & 1) * 4 + (i >> 1)), 0)
            ),
            scratch_shapes=[
                pltpu.VMEM((number, entries), BF16),
                pltpu.VMEM((rows, both), BF16),
                pltpu.VMEM((entries, tile), BF16),
                pltpu.VMEM((entries, tile), BF16),
                pltpu.VMEM((2, both, both), BF16),
                pltpu.VMEM((both, tile), F32),
                pltpu.VMEM((number, tile), F32),
                pltpu.SemaphoreType.DMA((2 + len(parts),)),
            ],
        ),
        out_shape=jax.ShapeDtypeStruct((rows, number), F32),
        compiler_params=pltpu.CompilerParams(vmem_limit_bytes=32 * MIB),
        cost_estimate=pl.CostEstimate(
            flops=2 * rows * number * entries, bytes_accessed=4 * rows * number, transcendentals=0
        ),
    )(place, sums, near, far, *parts)


def shards(inputs, cotangents, sketch_maps, lengths, queries):
    line = jnp.concatenate([queries] + [exchange(queries, 8 * d, 0) for d in (1, 2, 3)])
    near = jnp.concatenate([line] + [exchange(line, 2 * d, 0) for d in (1, 2, 3)])
    far = exchange(near, 1, 0)
    sides, part = sides_and_sums(inputs, cotangents, sketch_maps, lengths)
    pair = jnp.concatenate([sides, exchange(sides, 0, 4)])
    parts = [pair] + [exchange(pair, 0, d) for d in (1, 2, 3)]
    sums = sum_over_all(part)
    place = jnp.stack([lax.axis_index("corpus"), lax.axis_index("query")]).astype(jnp.int32)
    return scores_of(place, sums, near, far, parts)


def solution(mesh):
    placed = (
        P(BOTH, None),
        P(BOTH, None),
        P(),
        P(BOTH),
        P(("query", "corpus"), None),
    )
    return jax.shard_map(
        shards, mesh=mesh, in_specs=placed, out_specs=P("corpus", "query"), check_vma=False
    )
```

time: 221 us -> 108 us (0.49)
  blocking collectives: 87.2 us -> 0 us
  other arithmetic: 42.5 us -> 0.12 us
  starting transfers between devices: 0.09 us -> 32.2 us
  matrix products: 29.6 us -> 0 us
  Pallas kernels: 0 us -> 26.6 us
  between operations: 14.5 us -> 0.29 us
  local copies, waits for them, and re-layouts: 1.17 us -> 7.27 us
  waiting for transfers between devices: 44.4 us -> 41 us
    psum x1 -> x0, blocking collectives: 87.2 us -> none  [shards(): lax.psum((local_in, local_out, jnp.sum(live_mask)), ('corpus', 'query'))]
    all_gather x3 -> x0, waiting for transfers between devices: 44.4 us -> none  [the longest x1 44.3 us: shards(): conditioned = lax.all_gather(prepared, 'corpus', axis=0, tiled=True)]
    ppermute x0 -> x19, waiting for transfers between devices: none -> 41 us  [the longest x16 34.4 us: exchange(): return lax.ppermute(array, BOTH, pairs)]
    ppermute x0 -> x19, starting transfers between devices: none -> 32.2 us  [the longest x16 22.6 us: exchange(): return lax.ppermute(array, BOTH, pairs)]
    dot_general x7 -> x0, matrix products: 28.9 us -> none  [the longest x1 17.6 us: shards(): lax.dot_general(sketch, conditioned, (((1,), (1,)), ((), ())), preferred_...]
    pallas_call x0 -> x2, Pallas kernels: none -> 26.6 us  [the longest x1 21.9 us: scores_of(): pl.pallas_call(functools.partial(scores_kernel, tile=tile), grid_spec=plt...]
    another operation x10 -> x1, other arithmetic: 23.9 us -> 0.07 us  [shards(): jnp.stack([lax.axis_index('corpus'), lax.axis_index('query')])]
    convert_element_type x2 -> x0, other arithmetic: 14.6 us -> none  [the longest x1 13.8 us: shards(): sketch = (piece_out[:, :, None] * piece_in[:, None, :]).reshape(piece_row...]
  transfers between devices with their start and end apart: 3 -> 19, of which waited for: 1 -> 11; matrix products, arithmetic and copies ran while one was open for 23% -> 1% of each run, Pallas kernels for 0% -> 4%
where the time goes in v1:
time: 108 us; the launch traced here: 107 us
  waiting for transfers between devices  41 us (38%)
  starting transfers between devices  32.2 us (30%)
  Pallas kernels  26.6 us (25%)
  local copies, waits for them, and re-layouts  7.27 us (7%)
    ppermute x16, waiting for transfers between devices, exchange(): return lax.ppermute(array, BOTH, pairs)  34.4 us
    ppermute x16, starting transfers between devices, exchange(): return lax.ppermute(array, BOTH, pairs)  22.6 us
    pallas_call x1, Pallas kernels, scores_of(): pl.pallas_call(functools.partial(scores_kernel, tile=tile), grid_spec=plt...  21.9 us
    ppermute x3, starting transfers between devices, along_z(): return lax.ppermute(array, BOTH, pairs)  9.6 us
    unnamed x14, local copies, waits for them, and re-layouts  7.23 us
    ppermute x3, waiting for transfers between devices, along_z(): return lax.ppermute(array, BOTH, pairs)  6.54 us
    pallas_call x1, Pallas kernels, sides_and_sums(): pl.pallas_call(sides_kernel, grid_spec=pltpu.PrefetchScalarGridSpec(num_s...  4.63 us
  transfers between devices with their start and end apart: 19, of which 11 were waited for; matrix products, arithmetic and copies ran while one was open for 1% of the time, Pallas kernels for 4%

profile of v1, /device:TPU:24, one launch (start us, length us, event | category | flops | bytes accessed | tf_op | source)
XLA Modules:
  0.0 107.5 jit_solution(13313875310071488806)
XLA Ops:
  0.0 3.3 %collective-permute-start.9 = (bf16[8,4096]{1,0:T(8,128)(2,1)}, bf16[8,4096]{1,0:T(8,128)(2,1)S(1)}, u32[]{:S(2)}, u32[]{:S(2)}) collective-permute-start(bf16[8,4096]{1,0:T(8,128)(2,1)} %param.9), channel_id=1, source_target_pairs={{0,128},{1,129},{2,130},{3,131},{4,132},{5,133},{6,134},{7,135},{8... | collective-permute-start | bytes 196616 | tf_op jit(solution)/shard_map/ppermute | solution.py:24
  3.3 1.9 %collective-permute-start.8 = (bf16[8,4096]{1,0:T(8,128)(2,1)}, bf16[8,4096]{1,0:T(8,128)(2,1)S(1)}, u32[]{:S(2)}, u32[]{:S(2)}) collective-permute-start(bf16[8,4096]{1,0:T(8,128)(2,1)} %param.9), channel_id=1, source_target_pairs={{0,64},{1,65},{2,66},{3,67},{4,68},{5,69},{6,70},{7,71},{8,72},{9,... | collective-permute-start | bytes 196616 | tf_op jit(solution)/shard_map/ppermute | solution.py:24
  5.2 0.9 constant_dynamic-update-slice_fusion.3
  6.1 1.6 %collective-permute-done.8 = bf16[8,4096]{1,0:T(8,128)(2,1)S(1)} collective-permute-done((bf16[8,4096]{1,0:T(8,128)(2,1)}, bf16[8,4096]{1,0:T(8,128)(2,1)S(1)}, u32[]{:S(2)}, u32[]{:S(2)}) %collective-permute-start.8) | collective-permute-done | bytes 65568 | tf_op jit(solution)/shard_map/ppermute | solution.py:24
  7.8 3.7 %collective-permute-done.10 = bf16[8,4096]{1,0:T(8,128)(2,1)S(1)} collective-permute-done((bf16[8,4096]{1,0:T(8,128)(2,1)}, bf16[8,4096]{1,0:T(8,128)(2,1)S(1)}, u32[]{:S(2)}, u32[]{:S(2)}) %collective-permute-start.10) | collective-permute-done | bytes 65568 | tf_op jit(solution)/shard_map/ppermute | solution.py:24
  11.5 1.6 %collective-permute-start.11 = (bf16[32,4096]{1,0:T(8,128)(2,1)S(1)}, bf16[32,4096]{1,0:T(8,128)(2,1)S(1)}, u32[]{:S(2)}, u32[]{:S(2)}) collective-permute-start(bf16[32,4096]{1,0:T(8,128)(2,1)S(1)} %get-tuple-element.9), channel_id=1, source_target_pairs={{0,16},{1,17},{2,18},{3,19},{4,20},{5,21},{6,22},{7,23},{8,24},{9,... | collective-permute-start | bytes 786440 | tf_op jit(solution)/shard_map/ppermute | solution.py:24
  13.1 2.1 %collective-permute-start.13 = (bf16[32,4096]{1,0:T(8,128)(2,1)S(1)}, bf16[32,4096]{1,0:T(8,128)(2,1)S(1)}, u32[]{:S(2)}, u32[]{:S(2)}) collective-permute-start(bf16[32,4096]{1,0:T(8,128)(2,1)S(1)} %get-tuple-element.9), channel_id=1, source_target_pairs={{0,48},{1,49},{2,50},{3,51},{4,52},{5,53},{6,54},{7,55},{8,56},{9,... | collective-permute-start | bytes 786440 | tf_op jit(solution)/shard_map/ppermute | solution.py:24
  15.2 0.6 collective-permute-start.12
  15.8 4.8 %collective-permute-done.11 = bf16[32,4096]{1,0:T(8,128)(2,1)S(1)} collective-permute-done((bf16[32,4096]{1,0:T(8,128)(2,1)S(1)}, bf16[32,4096]{1,0:T(8,128)(2,1)S(1)}, u32[]{:S(2)}, u32[]{:S(2)}) %collective-permute-start.11) | collective-permute-done | bytes 262176 | tf_op jit(solution)/shard_map/ppermute | solution.py:24
  20.6 5.3 %collective-permute-done.12 = bf16[32,4096]{1,0:T(8,128)(2,1)S(1)} collective-permute-done((bf16[32,4096]{1,0:T(8,128)(2,1)S(1)}, bf16[32,4096]{1,0:T(8,128)(2,1)S(1)}, u32[]{:S(2)}, u32[]{:S(2)}) %collective-permute-start.12) | collective-permute-done | bytes 262176 | tf_op jit(solution)/shard_map/ppermute | solution.py:24
  26.2 2.2 %copy-done = bf16[512,4096]{1,0:T(8,128)(2,1)S(1)} copy-done((bf16[512,4096]{1,0:T(8,128)(2,1)S(1)}, bf16[512,4096]{1,0:T(8,128)(2,1)}, u32[]{:S(2)}) %copy-start) | copy-done | bytes 4194328
  28.4 2.2 %copy-done.1 = bf16[512,4096]{1,0:T(8,128)(2,1)S(1)} copy-done((bf16[512,4096]{1,0:T(8,128)(2,1)S(1)}, bf16[512,4096]{1,0:T(8,128)(2,1)}, u32[]{:S(2)}) %copy-start.1) | copy-done | bytes 4194328
  30.6 1.2 %copy-done.2 = bf16[4096,128]{1,0:T(8,128)(2,1)S(1)} copy-done((bf16[4096,128]{1,0:T(8,128)(2,1)S(1)}, bf16[4096,128]{1,0:T(8,128)(2,1)}, u32[]{:S(2)}) %copy-start.2) | copy-done | bytes 1048600
  31.8 0.7 copy-done.3
  32.4 4.6 %shard_map.55 = (bf16[512,128]{1,0:T(8,128)(2,1)S(1)}, f32[72,128]{1,0:T(8,128)S(1)}) custom-call(s32[4]{0:T(128)S(1)} %copy-done.3, bf16[512,4096]{1,0:T(8,128)(2,1)S(1)} %copy-done, bf16[512,4096]{1,0:T(8,128)(2,1)S(1)} %copy-done.1, bf16[4096,128]{1,0:T(8,128)(2,1)S(1)} %copy-done.2), custom_call_target="tpu_custom_call" | custom-call | flops 1073741824 | bytes 8388608 | tf_op jit(solution)/shard_map/pallas_call | solution.py:75
  37.1 0.6 collective-permute-start
  37.7 4.9 %collective-permute-start.15 = (bf16[512,128]{1,0:T(8,128)(2,1)S(1)}, bf16[512,128]{1,0:T(8,128)(2,1)S(1)}, u32[]{:S(2)}, u32[]{:S(2)}) collective-permute-start(bf16[512,128]{1,0:T(8,128)(2,1)S(1)} %get-tuple-element.8), channel_id=1, source_target_pairs={{0,4},{1,5},{2,6},{3,7},{4,0},{5,1},{6,2},{7,3},{8,12},{9,13},{10,... | collective-permute-start | bytes 393224 | tf_op jit(solution)/shard_map/ppermute | solution.py:24
  42.7 3.9 %collective-permute-done.1 = f32[72,128]{1,0:T(8,128)S(1)} collective-permute-done((f32[72,128]{1,0:T(8,128)S(1)}, f32[72,128]{1,0:T(8,128)S(1)}, u32[]{:S(2)}, u32[]{:S(2)}) %collective-permute-start.1) | collective-permute-done | bytes 36896 | tf_op jit(solution)/shard_map/ppermute | solution.py:24
  46.6 2.1 %collective-permute-start.2 = (f32[72,128]{1,0:T(8,128)S(1)}, f32[72,128]{1,0:T(8,128)S(1)}, u32[]{:S(2)}, u32[]{:S(2)}) collective-permute-start(f32[72,128]{1,0:T(8,128)S(1)} %add.25), channel_id=1, source_target_pairs={{0,48},{1,49},{2,50},{3,51},{4,52},{5,53},{6,54},{7,55},{8,56},{9,... | collective-permute-start | bytes 110600 | tf_op jit(solution)/shard_map/ppermute | solution.py:24
  49.0 2.6 %collective-permute-start.17 = (bf16[1024,128]{1,0:T(8,128)(2,1)S(1)}, bf16[1024,128]{1,0:T(8,128)(2,1)S(1)}, u32[]{:S(2)}, u32[]{:S(2)}) collective-permute-start(bf16[1024,128]{1,0:T(8,128)(2,1)S(1)} %constant_dynamic-update-slice_fusion.11.rest_0_), channel_id=1, source_target_pairs={{0,2},{1,3},{2,0},{3,1},{4,6},{5,7},{6,4},{7,5},{8,10},{9,11},{10,... | collective-permute-start | bytes 786440 | tf_op jit(solution)/shard_map/ppermute | solution.py:24
  51.6 1.3 %collective-permute-start.16 = (bf16[1024,128]{1,0:T(8,128)(2,1)S(1)}, bf16[1024,128]{1,0:T(8,128)(2,1)S(1)}, u32[]{:S(2)}, u32[]{:S(2)}) collective-permute-start(bf16[1024,128]{1,0:T(8,128)(2,1)S(1)} %constant_dynamic-update-slice_fusion.11.rest_0_), channel_id=1, source_target_pairs={{0,1},{1,0},{2,3},{3,2},{4,5},{5,4},{6,7},{7,6},{8,9},{9,8},{10,11... | collective-permute-start | bytes 786440 | tf_op jit(solution)/shard_map/ppermute | solution.py:24
  52.9 0.8 collective-permute-start.3
  53.7 10.2 %collective-permute-done.3 = f32[72,128]{1,0:T(8,128)S(1)} collective-permute-done((f32[72,128]{1,0:T(8,128)S(1)}, f32[72,128]{1,0:T(8,128)S(1)}, u32[]{:S(2)}, u32[]{:S(2)}) %collective-permute-start.3) | collective-permute-done | bytes 36896 | tf_op jit(solution)/shard_map/ppermute | solution.py:24
  63.9 0.4 collective-permute-start.4
  64.3 4.8 %collective-permute-done.4 = f32[72,128]{1,0:T(8,128)S(1)} collective-permute-done((f32[72,128]{1,0:T(8,128)S(1)}, f32[72,128]{1,0:T(8,128)S(1)}, u32[]{:S(2)}, u32[]{:S(2)}) %collective-permute-start.4) | collective-permute-done | bytes 36896 | tf_op jit(solution)/shard_map/ppermute | solution.py:24
  69.1 2.2 %collective-permute-start.5 = (f32[72,128]{1,0:T(8,128)S(1)}, f32[72,128]{1,0:T(8,128)S(1)}, u32[]{:S(2)}, u32[]{:S(2)}) collective-permute-start(f32[72,128]{1,0:T(8,128)S(1)} %add.28), channel_id=1, source_target_pairs={{0,64},{1,65},{2,66},{3,67},{4,68},{5,69},{6,70},{7,71},{8,72},{9,... | collective-permute-start | bytes 110600 | tf_op jit(solution)/shard_map/ppermute | solution.py:33
  71.3 1.9 %collective-permute-done.5 = f32[72,128]{1,0:T(8,128)S(1)} collective-permute-done((f32[72,128]{1,0:T(8,128)S(1)}, f32[72,128]{1,0:T(8,128)S(1)}, u32[]{:S(2)}, u32[]{:S(2)}) %collective-permute-start.5) | collective-permute-done | bytes 36896 | tf_op jit(solution)/shard_map/ppermute | solution.py:33
  73.3 4.4 %collective-permute-start.6 = (f32[72,128]{1,0:T(8,128)S(1)}, f32[72,128]{1,0:T(8,128)S(1)}, u32[]{:S(2)}, u32[]{:S(2)}) collective-permute-start(f32[72,128]{1,0:T(8,128)S(1)} %add.29), channel_id=1, source_target_pairs={{0,196},{1,197},{2,198},{3,199},{4,192},{5,193},{6,194},{7,195},{8... | collective-permute-start | bytes 110600 | tf_op jit(solution)/shard_map/ppermute | solution.py:33
  77.6 1.9 %collective-permute-done.6 = f32[72,128]{1,0:T(8,128)S(1)} collective-permute-done((f32[72,128]{1,0:T(8,128)S(1)}, f32[72,128]{1,0:T(8,128)S(1)}, u32[]{:S(2)}, u32[]{:S(2)}) %collective-permute-start.6) | collective-permute-done | bytes 36896 | tf_op jit(solution)/shard_map/ppermute | solution.py:33
  79.6 3.0 %collective-permute-start.7 = (f32[72,128]{1,0:T(8,128)S(1)}, f32[72,128]{1,0:T(8,128)S(1)}, u32[]{:S(2)}, u32[]{:S(2)}) collective-permute-start(f32[72,128]{1,0:T(8,128)S(1)} %add.30), channel_id=1, source_target_pairs={{0,192},{1,193},{2,194},{3,195},{4,196},{5,197},{6,198},{7,199},{8... | collective-permute-start | bytes 110600 | tf_op jit(solution)/shard_map/ppermute | solution.py:33
  82.7 2.7 %collective-permute-done.7 = f32[72,128]{1,0:T(8,128)S(1)} collective-permute-done((f32[72,128]{1,0:T(8,128)S(1)}, f32[72,128]{1,0:T(8,128)S(1)}, u32[]{:S(2)}, u32[]{:S(2)}) %collective-permute-start.7) | collective-permute-done | bytes 36896 | tf_op jit(solution)/shard_map/ppermute | solution.py:33
  85.4 21.9 %shard_map.56 = f32[4096,256]{1,0:T(8,128)} custom-call(s32[2]{0:T(128)S(1)} %pad_add_fusion.place_ref, f32[72,128]{1,0:T(8,128)S(1)} %add.31.sums_ref, bf16[128,4096]{1,0:T(8,128)(2,1)S(1)} %constant_dynamic-update-slice_fusion.4.near_ref, bf16[128,4096]{1,0:T(8,128)(2,1)S(1)} %collective-permute-done.14.far_ref, ...), custom_call_target="tpu_custom_call" | custom-call | flops 8589934592 | bytes 4194304 | tf_op jit(solution)/shard_map/pallas_call | solution.py:180
  (34 shorter events, 0.9 us)
Async XLA Ops:
  0.0 7.8 %collective-permute-start.9 = (bf16[8,4096]{1,0:T(8,128)(2,1)}, bf16[8,4096]{1,0:T(8,128)(2,1)S(1)}, u32[]{:S(2)}, u32[]{:S(2)}) collective-permute-start(bf16[8,4096]{1,0:T(8,128)(2,1)} %param.9), channel_id=1, source_target_pairs={{0,128},{1,129},{2,130},{3,131},{4,132},{5,133},{6,134},{7,135},{8... | collective-permute-start | bytes 196616 | tf_op jit(solution)/shard_map/ppermute | solution.py:24
  3.3 4.5 %collective-permute-start.8 = (bf16[8,4096]{1,0:T(8,128)(2,1)}, bf16[8,4096]{1,0:T(8,128)(2,1)S(1)}, u32[]{:S(2)}, u32[]{:S(2)}) collective-permute-start(bf16[8,4096]{1,0:T(8,128)(2,1)} %param.9), channel_id=1, source_target_pairs={{0,64},{1,65},{2,66},{3,67},{4,68},{5,69},{6,70},{7,71},{8,72},{9,... | collective-permute-start | bytes 196616 | tf_op jit(solution)/shard_map/ppermute | solution.py:24
  5.2 6.3 %collective-permute-start.10 = (bf16[8,4096]{1,0:T(8,128)(2,1)}, bf16[8,4096]{1,0:T(8,128)(2,1)S(1)}, u32[]{:S(2)}, u32[]{:S(2)}) collective-permute-start(bf16[8,4096]{1,0:T(8,128)(2,1)} %param.9), channel_id=1, source_target_pairs={{0,192},{1,193},{2,194},{3,195},{4,196},{5,197},{6,198},{7,199},{8... | collective-permute-start | bytes 196616 | tf_op jit(solution)/shard_map/ppermute | solution.py:24
  11.5 9.1 %collective-permute-start.11 = (bf16[32,4096]{1,0:T(8,128)(2,1)S(1)}, bf16[32,4096]{1,0:T(8,128)(2,1)S(1)}, u32[]{:S(2)}, u32[]{:S(2)}) collective-permute-start(bf16[32,4096]{1,0:T(8,128)(2,1)S(1)} %get-tuple-element.9), channel_id=1, source_target_pairs={{0,16},{1,17},{2,18},{3,19},{4,20},{5,21},{6,22},{7,23},{8,24},{9,... | collective-permute-start | bytes 786440 | tf_op jit(solution)/shard_map/ppermute | solution.py:24
  13.1 13.0 %collective-permute-start.13 = (bf16[32,4096]{1,0:T(8,128)(2,1)S(1)}, bf16[32,4096]{1,0:T(8,128)(2,1)S(1)}, u32[]{:S(2)}, u32[]{:S(2)}) collective-permute-start(bf16[32,4096]{1,0:T(8,128)(2,1)S(1)} %get-tuple-element.9), channel_id=1, source_target_pairs={{0,48},{1,49},{2,50},{3,51},{4,52},{5,53},{6,54},{7,55},{8,56},{9,... | collective-permute-start | bytes 786440 | tf_op jit(solution)/shard_map/ppermute | solution.py:24
  15.2 10.8 %collective-permute-start.12 = (bf16[32,4096]{1,0:T(8,128)(2,1)S(1)}, bf16[32,4096]{1,0:T(8,128)(2,1)S(1)}, u32[]{:S(2)}, u32[]{:S(2)}) collective-permute-start(bf16[32,4096]{1,0:T(8,128)(2,1)S(1)} %get-tuple-element.9), channel_id=1, source_target_pairs={{0,32},{1,33},{2,34},{3,35},{4,36},{5,37},{6,38},{7,39},{8,40},{9,... | collective-permute-start | bytes 786440 | tf_op jit(solution)/shard_map/ppermute | solution.py:24
  26.1 59.3 %collective-permute-start.14 = (bf16[128,4096]{1,0:T(8,128)(2,1)S(1)}, bf16[128,4096]{1,0:T(8,128)(2,1)S(1)}, u32[]{:S(2)}, u32[]{:S(2)}) collective-permute-start(bf16[128,4096]{1,0:T(8,128)(2,1)S(1)} %constant_dynamic-update-slice_fusion.4.near_ref), channel_id=1, source_target_pairs={{0,8},{1,9},{2,10},{3,11},{4,12},{5,13},{6,14},{7,15},{8,0},{9,1},... | collective-permute-start | bytes 3145736 | tf_op jit(solution)/shard_map/ppermute | solution.py:24
  26.2 2.2 %copy-start = (bf16[512,4096]{1,0:T(8,128)(2,1)S(1)}, bf16[512,4096]{1,0:T(8,128)(2,1)}, u32[]{:S(2)}) copy-start(bf16[512,4096]{1,0:T(8,128)(2,1)} %inputs_ref.1) | copy-start | bytes 12582916
  28.4 2.2 %copy-start.1 = (bf16[512,4096]{1,0:T(8,128)(2,1)S(1)}, bf16[512,4096]{1,0:T(8,128)(2,1)}, u32[]{:S(2)}) copy-start(bf16[512,4096]{1,0:T(8,128)(2,1)} %cotangents_ref.1) | copy-start | bytes 12582916
  30.5 1.2 %copy-start.2 = (bf16[4096,128]{1,0:T(8,128)(2,1)S(1)}, bf16[4096,128]{1,0:T(8,128)(2,1)}, u32[]{:S(2)}) copy-start(bf16[4096,128]{1,0:T(8,128)(2,1)} %maps_ref.1) | copy-start | bytes 3145732
  31.8 0.7 copy-start.3
  37.1 5.4 %collective-permute-start = (f32[72,128]{1,0:T(8,128)S(1)}, f32[72,128]{1,0:T(8,128)S(1)}, u32[]{:S(2)}, u32[]{:S(2)}) collective-permute-start(f32[72,128]{1,0:T(8,128)S(1)} %get-tuple-element.7), channel_id=1, source_target_pairs={{0,8},{1,9},{2,10},{3,11},{4,12},{5,13},{6,14},{7,15},{8,0},{9,1},... | collective-permute-start | bytes 110600 | tf_op jit(solution)/shard_map/ppermute | solution.py:24
  37.7 11.0 %collective-permute-start.15 = (bf16[512,128]{1,0:T(8,128)(2,1)S(1)}, bf16[512,128]{1,0:T(8,128)(2,1)S(1)}, u32[]{:S(2)}, u32[]{:S(2)}) collective-permute-start(bf16[512,128]{1,0:T(8,128)(2,1)S(1)} %get-tuple-element.8), channel_id=1, source_target_pairs={{0,4},{1,5},{2,6},{3,7},{4,0},{5,1},{6,2},{7,3},{8,12},{9,13},{10,... | collective-permute-start | bytes 393224 | tf_op jit(solution)/shard_map/ppermute | solution.py:24
  42.5 4.0 %collective-permute-start.1 = (f32[72,128]{1,0:T(8,128)S(1)}, f32[72,128]{1,0:T(8,128)S(1)}, u32[]{:S(2)}, u32[]{:S(2)}) collective-permute-start(f32[72,128]{1,0:T(8,128)S(1)} %add.24), channel_id=1, source_target_pairs={{0,16},{1,17},{2,18},{3,19},{4,20},{5,21},{6,22},{7,23},{8,24},{9,... | collective-permute-start | bytes 110600 | tf_op jit(solution)/shard_map/ppermute | solution.py:24
  46.6 6.3 %collective-permute-start.2 = (f32[72,128]{1,0:T(8,128)S(1)}, f32[72,128]{1,0:T(8,128)S(1)}, u32[]{:S(2)}, u32[]{:S(2)}) collective-permute-start(f32[72,128]{1,0:T(8,128)S(1)} %add.25), channel_id=1, source_target_pairs={{0,48},{1,49},{2,50},{3,51},{4,52},{5,53},{6,54},{7,55},{8,56},{9,... | collective-permute-start | bytes 110600 | tf_op jit(solution)/shard_map/ppermute | solution.py:24
  48.7 36.6 %collective-permute-start.18 = (bf16[1024,128]{1,0:T(8,128)(2,1)S(1)}, bf16[1024,128]{1,0:T(8,128)(2,1)S(1)}, u32[]{:S(2)}, u32[]{:S(2)}) collective-permute-start(bf16[1024,128]{1,0:T(8,128)(2,1)S(1)} %constant_dynamic-update-slice_fusion.11.rest_0_), channel_id=1, source_target_pairs={{0,3},{1,2},{2,1},{3,0},{4,7},{5,6},{6,5},{7,4},{8,11},{9,10},{10,... | collective-permute-start | bytes 786440 | tf_op jit(solution)/shard_map/ppermute | solution.py:24
  49.0 36.3 %collective-permute-start.17 = (bf16[1024,128]{1,0:T(8,128)(2,1)S(1)}, bf16[1024,128]{1,0:T(8,128)(2,1)S(1)}, u32[]{:S(2)}, u32[]{:S(2)}) collective-permute-start(bf16[1024,128]{1,0:T(8,128)(2,1)S(1)} %constant_dynamic-update-slice_fusion.11.rest_0_), channel_id=1, source_target_pairs={{0,2},{1,3},{2,0},{3,1},{4,6},{5,7},{6,4},{7,5},{8,10},{9,11},{10,... | collective-permute-start | bytes 786440 | tf_op jit(solution)/shard_map/ppermute | solution.py:24
  51.6 33.8 %collective-permute-start.16 = (bf16[1024,128]{1,0:T(8,128)(2,1)S(1)}, bf16[1024,128]{1,0:T(8,128)(2,1)S(1)}, u32[]{:S(2)}, u32[]{:S(2)}) collective-permute-start(bf16[1024,128]{1,0:T(8,128)(2,1)S(1)} %constant_dynamic-update-slice_fusion.11.rest_0_), channel_id=1, source_target_pairs={{0,1},{1,0},{2,3},{3,2},{4,5},{5,4},{6,7},{7,6},{8,9},{9,8},{10,11... | collective-permute-start | bytes 786440 | tf_op jit(solution)/shard_map/ppermute | solution.py:24
  52.9 11.0 %collective-permute-start.3 = (f32[72,128]{1,0:T(8,128)S(1)}, f32[72,128]{1,0:T(8,128)S(1)}, u32[]{:S(2)}, u32[]{:S(2)}) collective-permute-start(f32[72,128]{1,0:T(8,128)S(1)} %add.26), channel_id=1, source_target_pairs={{0,1},{1,0},{2,3},{3,2},{4,5},{5,4},{6,7},{7,6},{8,9},{9,8},{10,11... | collective-permute-start | bytes 110600 | tf_op jit(solution)/shard_map/ppermute | solution.py:24
  63.9 5.2 %collective-permute-start.4 = (f32[72,128]{1,0:T(8,128)S(1)}, f32[72,128]{1,0:T(8,128)S(1)}, u32[]{:S(2)}, u32[]{:S(2)}) collective-permute-start(f32[72,128]{1,0:T(8,128)S(1)} %add.27), channel_id=1, source_target_pairs={{0,3},{1,2},{2,1},{3,0},{4,7},{5,6},{6,5},{7,4},{8,11},{9,10},{10,... | collective-permute-start | bytes 110600 | tf_op jit(solution)/shard_map/ppermute | solution.py:24
  69.1 4.2 %collective-permute-start.5 = (f32[72,128]{1,0:T(8,128)S(1)}, f32[72,128]{1,0:T(8,128)S(1)}, u32[]{:S(2)}, u32[]{:S(2)}) collective-permute-start(f32[72,128]{1,0:T(8,128)S(1)} %add.28), channel_id=1, source_target_pairs={{0,64},{1,65},{2,66},{3,67},{4,68},{5,69},{6,70},{7,71},{8,72},{9,... | collective-permute-start | bytes 110600 | tf_op jit(solution)/shard_map/ppermute | solution.py:33
  73.3 6.3 %collective-permute-start.6 = (f32[72,128]{1,0:T(8,128)S(1)}, f32[72,128]{1,0:T(8,128)S(1)}, u32[]{:S(2)}, u32[]{:S(2)}) collective-permute-start(f32[72,128]{1,0:T(8,128)S(1)} %add.29), channel_id=1, source_target_pairs={{0,196},{1,197},{2,198},{3,199},{4,192},{5,193},{6,194},{7,195},{8... | collective-permute-start | bytes 110600 | tf_op jit(solution)/shard_map/ppermute | solution.py:33
  79.6 5.8 %collective-permute-start.7 = (f32[72,128]{1,0:T(8,128)S(1)}, f32[72,128]{1,0:T(8,128)S(1)}, u32[]{:S(2)}, u32[]{:S(2)}) collective-permute-start(f32[72,128]{1,0:T(8,128)S(1)} %add.30), channel_id=1, source_target_pairs={{0,192},{1,193},{2,194},{3,195},{4,196},{5,197},{6,198},{7,199},{8... | collective-permute-start | bytes 110600 | tf_op jit(solution)/shard_map/ppermute | solution.py:33

commit v2 on v1

v2 whole, which is shorter than its diff:
```python
import functools

import jax
import jax.numpy as jnp
from jax import lax
from jax.experimental import pallas as pl
from jax.experimental.pallas import tpu as pltpu
from jax.sharding import PartitionSpec as P

F32 = jnp.float32
BF16 = jnp.bfloat16
BOTH = ("corpus", "query")
NT = (((1,), (1,)), ((), ()))
TN = (((0,), (0,)), ((), ()))
MIB = 1 << 20
LIVE = 81920.0


def exchange(array, corpus_bits, query_bits):
    pairs = [
        (c * 8 + q, (c ^ corpus_bits) * 8 + (q ^ query_bits))
        for c in range(32)
        for q in range(8)
    ]
    return lax.ppermute(array, BOTH, pairs)


def along_z(array, partner):
    pairs = []
    for c in range(32):
        for q in range(8):
            z = partner[(q >> 2) * 4 + (c >> 3)]
            pairs.append((c * 8 + q, ((z & 3) * 8 + (c & 7)) * 8 + (z >> 2) * 4 + (q & 3)))
    return lax.ppermute(array, BOTH, pairs)


def sides_kernel(lengths_ref, inputs_ref, cotangents_ref, maps_ref, queries_ref, sides_ref, passed_ref,
                 read_in, read_out, maps, sem):
    rank = maps_ref.shape[1] // 2
    sequences = lengths_ref.shape[0]
    slots = inputs_ref.shape[0] // sequences
    first = pltpu.make_async_copy(maps_ref, maps, sem.at[2 * sequences])
    first.start()
    copies = []
    for s in range(sequences):
        rows = pl.ds(s * slots, slots)
        copies.append(pltpu.make_async_copy(inputs_ref.at[rows], read_in.at[rows], sem.at[2 * s]))
        copies.append(pltpu.make_async_copy(cotangents_ref.at[rows], read_out.at[rows], sem.at[2 * s + 1]))
    for copy in copies:
        copy.start()
    last = pltpu.make_async_copy(queries_ref, passed_ref, sem.at[2 * sequences + 1])
    last.start()
    first.wait()
    row = lax.broadcasted_iota(jnp.int32, (slots, 2 * rank), 0)
    lane = lax.broadcasted_iota(jnp.int32, (slots, 2 * rank), 1)
    for s in range(sequences):
        rows = pl.ds(s * slots, slots)
        copies[2 * s].wait()
        of_in = jnp.dot(read_in[rows], maps[...], preferred_element_type=F32)
        copies[2 * s + 1].wait()
        of_out = jnp.dot(read_out[rows], maps[...], preferred_element_type=F32)
        sides = jnp.where(row < lengths_ref[s], jnp.where(lane < rank, of_in, of_out), 0.0)
        sides_ref[rows] = sides.astype(BF16)
    last.wait()


def sides_of(inputs, cotangents, sketch_maps, lengths, queries):
    rows, width = inputs.shape
    both = sketch_maps.shape[1]
    sequences = lengths.shape[0]
    anywhere = pl.BlockSpec(memory_space=pl.ANY)
    return pl.pallas_call(
        sides_kernel,
        in_specs=[pl.BlockSpec(memory_space=pltpu.SMEM)] + [anywhere] * 4,
        out_specs=[pl.BlockSpec(memory_space=pltpu.VMEM)] * 2,
        scratch_shapes=[
            pltpu.VMEM((rows, width), BF16),
            pltpu.VMEM((rows, width), BF16),
            pltpu.VMEM((width, both), BF16),
            pltpu.SemaphoreType.DMA((2 * sequences + 2,)),
        ],
        out_shape=[
            jax.ShapeDtypeStruct((rows, both), BF16),
            jax.ShapeDtypeStruct(queries.shape, BF16),
        ],
        compiler_params=pltpu.CompilerParams(vmem_limit_bytes=56 * MIB),
        cost_estimate=pl.CostEstimate(
            flops=4 * rows * width * both, bytes_accessed=4 * rows * width, transcendentals=0
        ),
    )(lengths, inputs, cotangents, sketch_maps, queries)


def moments_kernel(*refs):
    *parts, out_ref = refs
    rank = out_ref.shape[0]
    total = jnp.zeros((2 * rank, 2 * rank), F32)
    for part in parts:
        total += lax.dot_general(part[...], part[...], TN, preferred_element_type=F32)
    lane = lax.broadcasted_iota(jnp.int32, out_ref.shape, 1)
    out_ref[...] = jnp.where(lane < rank, total[:rank], total[rank:])


def moments_of(parts):
    both = parts[0].shape[1]
    vmem = pl.BlockSpec(memory_space=pltpu.VMEM)
    return pl.pallas_call(
        moments_kernel,
        in_specs=[vmem] * len(parts),
        out_specs=vmem,
        out_shape=jax.ShapeDtypeStruct((both // 2, both), F32),
        compiler_params=pltpu.CompilerParams(vmem_limit_bytes=16 * MIB),
    )(*parts)


def damped_inverses(sums):
    rank = sums.shape[0]
    shape = (rank, 2 * rank)
    row = lax.broadcasted_iota(jnp.int32, shape, 0)
    lane = lax.broadcasted_iota(jnp.int32, shape, 1)
    left = lane < rank
    column = jnp.where(left, lane, lane - rank)
    moment = sums / LIVE
    diagonal = jnp.where(row == column, moment, 0.0)
    trace_in = jnp.sum(jnp.where(left, diagonal, 0.0))
    trace_out = jnp.sum(jnp.where(left, 0.0, diagonal))
    damping = 0.1 / rank * jnp.where(left, trace_in, trace_out)
    work = moment + jnp.where(row == column, damping, 0.0)
    size = 8
    within = lax.broadcasted_iota(jnp.int32, (size, 2 * rank), 0)
    for first in range(0, rank, size):
        wide = [
            jnp.where(left, work[:, k : k + 1], work[:, rank + k : rank + k + 1])
            for k in range(first, first + size)
        ]
        offset = column - first
        inside = (offset >= 0) & (offset < size)
        pivots = [w[first : first + size] for w in wide]
        rows = jnp.where(inside[:size], jnp.where(offset[:size] == within, 1.0, 0.0), work[first : first + size])
        for k in range(size):
            inverse = reciprocal(pivots[k][k : k + 1])
            factor = jnp.where(within == k, 0.0, pivots[k])
            own = rows[k : k + 1] * inverse
            rows = jnp.where(within == k, own, rows - factor * own)
            for later in range(k + 1, size):
                own = pivots[later][k : k + 1] * inverse
                pivots[later] = jnp.where(within == k, own, pivots[later] - factor * own)
        rest = jnp.where(inside, 0.0, work)
        for k in range(size):
            rest = rest - wide[k] * rows[k : k + 1]
        work = jnp.concatenate(
            [rows if k == first else rest[k : k + size] for k in range(0, rank, size)]
        )
    return work


def reciprocal(value):
    guess = pl.reciprocal(value, approx=True)
    guess = guess * (2.0 - value * guess)
    return guess * (2.0 - value * guess)


def scores_kernel(place_ref, sums_ref, near_ref, far_ref, *rest, tile, together):
    *parts, out_ref, held, blocks, sketches, lhs, turned, moved, ready, in_sem, out_sem = rest
    rank = sums_ref.shape[0]
    near = near_ref.shape[0]
    part = parts[0].shape[0]
    tiles = blocks.shape[0] // tile
    rounds = tiles // together

    def build(index, into):
        own = turned.at[index]
        of_in = own[:rank, :]
        for i in range(rank):
            into[i * rank : (i + 1) * rank, :] = (own[rank + i : rank + i + 1, :] * of_in).astype(BF16)

    def score(sketch, moved):
        product = jnp.dot(held[...], sketch[...], preferred_element_type=F32)
        for slot in range(product.shape[0] // 8):
            difference = (slot & 3) * 8 + ((slot >> 2) & 3) * 2 + (slot >> 4)
            target = pl.multiple_of((place_ref[0] ^ difference) * 8, 8)
            moved[pl.ds(target, 8), :] = product[slot * 8 : (slot + 1) * 8, :]
        return moved[...].T

    copies = [
        pltpu.make_async_copy(near_ref, held.at[pl.ds(0, near), :], in_sem.at[0]),
        pltpu.make_async_copy(far_ref, held.at[pl.ds(near, near), :], in_sem.at[1]),
    ]
    for i, ref in enumerate(parts):
        copies.append(pltpu.make_async_copy(ref, blocks.at[pl.ds(i * part, part), :], in_sem.at[2 + i]))
    for copy in copies:
        copy.start()
    inverses = damped_inverses(sums_ref[...])
    left = lax.broadcasted_iota(jnp.int32, inverses.shape, 1) < rank
    whole = jnp.concatenate([jnp.where(left, inverses, 0.0), jnp.where(left, 0.0, inverses)])
    high = whole.astype(BF16)
    lhs[: 2 * rank, :] = high
    lhs[2 * rank :, :] = (whole - high.astype(F32)).astype(BF16)
    for copy in copies:
        copy.wait()
    for index in range(tiles):
        sides = blocks[index * tile : (index + 1) * tile, :]
        both = lax.dot_general(lhs[...], sides, NT, preferred_element_type=F32)
        turned[index] = both[: 2 * rank] + both[2 * rank :]
    build(0, sketches[0])

    def written(round_, h):
        index = round_ * together + h
        slot = index // (part // 2 // tile)
        block = place_ref[1] ^ ((slot & 1) * 4 + (slot >> 1))
        row = block * (part // 2) + (index % (part // 2 // tile)) * tile
        buffer = (round_ % 2) * together + h
        return pltpu.make_async_copy(
            ready.at[buffer], out_ref.at[pl.ds(pl.multiple_of(row, tile), tile), :], out_sem.at[buffer]
        )

    @pl.loop(0, rounds)
    def _(round_):
        @pl.when(round_ >= 2)
        def _():
            for h in range(together):
                written(round_ - 2, h).wait()

        for h in range(together):
            ready[(round_ % 2) * together + h] = score(sketches[h % 2], moved[h % 2])
            build(jnp.minimum(round_ * together + h + 1, tiles - 1), sketches[(h + 1) % 2])
        for h in range(together):
            written(round_, h).start()

    for round_ in (rounds - 2, rounds - 1):
        for h in range(together):
            written(round_, h).wait()


def scores_of(place, sums, near, far, parts, tile=256, together=4):
    both = sums.shape[1]
    number, entries = 2 * near.shape[0], near.shape[1]
    rows = sum(part.shape[0] for part in parts)
    anywhere = pl.BlockSpec(memory_space=pl.ANY)
    return pl.pallas_call(
        functools.partial(scores_kernel, tile=tile, together=together),
        in_specs=[pl.BlockSpec(memory_space=pltpu.SMEM), pl.BlockSpec(memory_space=pltpu.VMEM)]
        + [anywhere] * (2 + len(parts)),
        out_specs=anywhere,
        scratch_shapes=[
            pltpu.VMEM((number, entries), BF16),
            pltpu.VMEM((rows, both), BF16),
            [pltpu.VMEM((entries, tile), BF16)] * 2,
            pltpu.VMEM((2 * both, both), BF16),
            pltpu.VMEM((rows // tile, both, tile), F32),
            [pltpu.VMEM((number, tile), F32)] * 2,
            pltpu.VMEM((2 * together, tile, number), F32),
            pltpu.SemaphoreType.DMA((2 + len(parts),)),
            pltpu.SemaphoreType.DMA((2 * together,)),
        ],
        out_shape=jax.ShapeDtypeStruct((rows, number), F32),
        compiler_params=pltpu.CompilerParams(vmem_limit_bytes=32 * MIB),
        cost_estimate=pl.CostEstimate(
            flops=2 * rows * number * entries, bytes_accessed=4 * rows * number, transcendentals=0
        ),
    )(place, sums, near, far, *parts)


def shards(inputs, cotangents, sketch_maps, lengths, queries):
    sides, queries = sides_of(inputs, cotangents, sketch_maps, lengths, queries)
    pair = jnp.concatenate([sides, exchange(sides, 0, 4)])
    line = jnp.concatenate([queries] + [exchange(queries, 8 * d, 0) for d in (1, 2, 3)])
    pair, line = lax.optimization_barrier((pair, line))
    parts = [pair] + [exchange(pair, 0, d) for d in (1, 2, 3)]
    lines = [line] + [exchange(line, 2 * d, 0) for d in (1, 2, 3)]
    sums = moments_of(parts)
    for d in (1, 8, 16):
        sums = sums + exchange(sums, d, 0)
    *lines, sums = lax.optimization_barrier((*lines, sums))
    sums = sums + (exchange(sums, 2, 0) + exchange(sums, 4, 0) + exchange(sums, 6, 0))
    near = jnp.concatenate(lines)
    far = exchange(near, 1, 0)
    place = jnp.stack([lax.axis_index("corpus"), lax.axis_index("query")]).astype(jnp.int32)
    return scores_of(place, sums, near, far, parts)


def solution(mesh):
    placed = (
        P(BOTH, None),
        P(BOTH, None),
        P(),
        P(BOTH),
        P(("query", "corpus"), None),
    )
    return jax.shard_map(
        shards, mesh=mesh, in_specs=placed, out_specs=P("corpus", "query"), check_vma=False
    )
```

time: 108 us -> 76 us (0.70)
  waiting for transfers between devices: 41 us -> 21.6 us
  local copies, waits for them, and re-layouts: 7.27 us -> 0.08 us
  Pallas kernels: 26.6 us -> 22.1 us
  starting transfers between devices: 32.2 us -> 29.9 us
  other arithmetic: 0.12 us -> 1.88 us
    ppermute x16 -> x17, waiting for transfers between devices: 34.4 us -> 21.6 us  [exchange(): return lax.ppermute(array, BOTH, pairs)]
    ppermute x3 -> x0, starting transfers between devices: 9.6 us -> none  [along_z(): return lax.ppermute(array, BOTH, pairs)]
    ppermute x16 -> x17, starting transfers between devices: 22.6 us -> 29.9 us  [exchange(): return lax.ppermute(array, BOTH, pairs)]
    unnamed x14 -> x3, local copies, waits for them, and re-layouts: 7.23 us -> 0.06 us
    ppermute x3 -> x0, waiting for transfers between devices: 6.54 us -> none  [along_z(): return lax.ppermute(array, BOTH, pairs)]
    pallas_call x2 -> x3, Pallas kernels: 26.6 us -> 22.1 us  [the longest x1 15.3 us: scores_of(): pl.pallas_call(functools.partial(scores_kernel, tile=tile, together=toget...]
    concatenate x0 -> x2, other arithmetic: none -> 1.78 us  [the longest x1 0.92 us: shards(): pair = jnp.concatenate([sides, exchange(sides, 0, 4)])]
  transfers between devices with their start and end apart: 19 -> 17, of which waited for: 11 -> 7; matrix products, arithmetic and copies ran while one was open for 1% -> 1% of each run, Pallas kernels for 4% -> 1%
where the time goes in v2:
time: 76 us; the launch traced here: 75.9 us
  starting transfers between devices  29.9 us (39%)
  Pallas kernels  22.1 us (29%)
  waiting for transfers between devices  21.6 us (28%)
  other arithmetic  1.88 us (2%)
    ppermute x17, starting transfers between devices, exchange(): return lax.ppermute(array, BOTH, pairs)  29.9 us
    ppermute x17, waiting for transfers between devices, exchange(): return lax.ppermute(array, BOTH, pairs)  21.6 us
    pallas_call x1, Pallas kernels, scores_of(): pl.pallas_call(functools.partial(scores_kernel, tile=tile, together=toget...  15.3 us
    pallas_call x1, Pallas kernels, sides_of(): pl.pallas_call(sides_kernel, in_specs=[pl.BlockSpec(memory_space=pltpu.SM...  6.37 us
  transfers between devices with their start and end apart: 17, of which 7 were waited for; matrix products, arithmetic and copies ran while one was open for 1% of the time, Pallas kernels for 1%

profile of v2, /device:TPU:24, one launch (start us, length us, event | category | flops | bytes accessed | tf_op | source)
XLA Modules:
  0.0 75.9 jit_solution(13139290728542416988)
XLA Ops:
  0.0 6.4 %shard_map.55 = (bf16[512,128]{1,0:T(8,128)(2,1)}, bf16[8,4096]{1,0:T(8,128)(2,1)}) custom-call(s32[4]{0:T(128)} %lengths_ref.1, bf16[512,4096]{1,0:T(8,128)(2,1)} %inputs_ref.1, bf16[512,4096]{1,0:T(8,128)(2,1)} %cotangents_ref.1, bf16[4096,128]{1,0:T(8,128)(2,1)} %maps_ref.1, bf16[8,4096]{1,0:T(8,128)(2,1)} %queries_ref.1), custom_call_target="tpu_custom_call" | custom-call | flops 1073741824 | bytes 8388608 | tf_op jit(solution)/shard_map/pallas_call | solution.py:72
  6.4 4.7 %collective-permute-start.3 = (bf16[8,4096]{1,0:T(8,128)(2,1)}, bf16[8,4096]{1,0:T(8,128)(2,1)S(1)}, u32[]{:S(2)}, u32[]{:S(2)}) collective-permute-start(bf16[8,4096]{1,0:T(8,128)(2,1)} %get-tuple-element.15), channel_id=1, source_target_pairs={{0,192},{1,193},{2,194},{3,195},{4,196},{5,197},{6,198},{7,199},{8... | collective-permute-start | bytes 196616 | tf_op jit(solution)/shard_map/ppermute | solution.py:25
  11.1 0.7 collective-permute-start.1
  11.8 6.3 %collective-permute-start = (bf16[512,128]{1,0:T(8,128)(2,1)}, bf16[512,128]{1,0:T(8,128)(2,1)S(1)}, u32[]{:S(2)}, u32[]{:S(2)}) collective-permute-start(bf16[512,128]{1,0:T(8,128)(2,1)} %get-tuple-element.14), channel_id=1, source_target_pairs={{0,4},{1,5},{2,6},{3,7},{4,0},{5,1},{6,2},{7,3},{8,12},{9,13},{10,... | collective-permute-start | bytes 393224 | tf_op jit(solution)/shard_map/ppermute | solution.py:25
  18.0 0.0 collective-permute-done.3
  18.0 0.0 collective-permute-done.2
  18.1 0.9 %pad_maximum_fusion.1 = bf16[32,4096]{1,0:T(8,128)(2,1)S(1)} fusion(bf16[8,4096]{1,0:T(8,128)(2,1)S(1)} %collective-permute-done.3, bf16[8,4096]{1,0:T(8,128)(2,1)S(1)} %collective-permute-done.2, bf16[8,4096]{1,0:T(8,128)(2,1)S(1)} %collective-permute-done.1, bf16[8,4096]{1,0:T(8,128)(2,1)} %get-tuple-element.15), kind=kLoop, calls=%fused_computation.1 | loop fusion | flops 1048576 | bytes 524288 | tf_op jit(solution)/shard_map/concatenate | solution.py:266
  18.9 6.3 %collective-permute-done = bf16[512,128]{1,0:T(8,128)(2,1)S(1)} collective-permute-done((bf16[512,128]{1,0:T(8,128)(2,1)}, bf16[512,128]{1,0:T(8,128)(2,1)S(1)}, u32[]{:S(2)}, u32[]{:S(2)}) %collective-permute-start) | collective-permute-done | bytes 131104 | tf_op jit(solution)/shard_map/ppermute | solution.py:25
  25.2 0.9 %pad_maximum_fusion.refs_0_.rest_0_ = bf16[1024,128]{1,0:T(8,128)(2,1)S(1)} fusion(bf16[512,128]{1,0:T(8,128)(2,1)S(1)} %collective-permute-done, bf16[512,128]{1,0:T(8,128)(2,1)} %get-tuple-element.14), kind=kLoop, calls=%fused_computation | loop fusion | flops 524288 | bytes 524288 | tf_op jit(solution)/shard_map/concatenate | solution.py:265
  26.1 0.3 collective-permute-start.9
  26.4 2.6 %collective-permute-start.8 = (bf16[1024,128]{1,0:T(8,128)(2,1)S(1)}, bf16[1024,128]{1,0:T(8,128)(2,1)S(1)}, u32[]{:S(2)}, u32[]{:S(2)}) collective-permute-start(bf16[1024,128]{1,0:T(8,128)(2,1)S(1)} %pad_maximum_fusion.refs_0_.rest_0_), channel_id=1, source_target_pairs={{0,2},{1,3},{2,0},{3,1},{4,6},{5,7},{6,4},{7,5},{8,10},{9,11},{10,... | collective-permute-start | bytes 786440 | tf_op jit(solution)/shard_map/ppermute | solution.py:25
  29.0 1.3 %collective-permute-start.7 = (bf16[1024,128]{1,0:T(8,128)(2,1)S(1)}, bf16[1024,128]{1,0:T(8,128)(2,1)S(1)}, u32[]{:S(2)}, u32[]{:S(2)}) collective-permute-start(bf16[1024,128]{1,0:T(8,128)(2,1)S(1)} %pad_maximum_fusion.refs_0_.rest_0_), channel_id=1, source_target_pairs={{0,1},{1,0},{2,3},{3,2},{4,5},{5,4},{6,7},{7,6},{8,9},{9,8},{10,11... | collective-permute-start | bytes 786440 | tf_op jit(solution)/shard_map/ppermute | solution.py:25
  30.3 2.8 %collective-permute-start.6 = (bf16[32,4096]{1,0:T(8,128)(2,1)S(1)}, bf16[32,4096]{1,0:T(8,128)(2,1)S(1)}, u32[]{:S(2)}, u32[]{:S(2)}) collective-permute-start(bf16[32,4096]{1,0:T(8,128)(2,1)S(1)} %pad_maximum_fusion.1), channel_id=1, source_target_pairs={{0,48},{1,49},{2,50},{3,51},{4,52},{5,53},{6,54},{7,55},{8,56},{9,... | collective-permute-start | bytes 786440 | tf_op jit(solution)/shard_map/ppermute | solution.py:25
  33.1 0.8 %collective-permute-start.5 = (bf16[32,4096]{1,0:T(8,128)(2,1)S(1)}, bf16[32,4096]{1,0:T(8,128)(2,1)S(1)}, u32[]{:S(2)}, u32[]{:S(2)}) collective-permute-start(bf16[32,4096]{1,0:T(8,128)(2,1)S(1)} %pad_maximum_fusion.1), channel_id=1, source_target_pairs={{0,32},{1,33},{2,34},{3,35},{4,36},{5,37},{6,38},{7,39},{8,40},{9,... | collective-permute-start | bytes 786440 | tf_op jit(solution)/shard_map/ppermute | solution.py:25
  33.9 6.1 %collective-permute-done.9.refs_3_.rest_3_ = bf16[1024,128]{1,0:T(8,128)(2,1)S(1)} collective-permute-done((bf16[1024,128]{1,0:T(8,128)(2,1)S(1)}, bf16[1024,128]{1,0:T(8,128)(2,1)S(1)}, u32[]{:S(2)}, u32[]{:S(2)}) %collective-permute-start.9) | collective-permute-done | bytes 262176 | tf_op jit(solution)/shard_map/ppermute | solution.py:25
  40.0 1.5 %collective-permute-start.4 = (bf16[32,4096]{1,0:T(8,128)(2,1)S(1)}, bf16[32,4096]{1,0:T(8,128)(2,1)S(1)}, u32[]{:S(2)}, u32[]{:S(2)}) collective-permute-start(bf16[32,4096]{1,0:T(8,128)(2,1)S(1)} %pad_maximum_fusion.1), channel_id=1, source_target_pairs={{0,16},{1,17},{2,18},{3,19},{4,20},{5,21},{6,22},{7,23},{8,24},{9,... | collective-permute-start | bytes 786440 | tf_op jit(solution)/shard_map/ppermute | solution.py:25
  41.5 0.5 shard_map.56
  42.0 0.1 collective-permute-start.10
  42.1 1.2 %collective-permute-done.10 = f32[64,128]{1,0:T(8,128)S(1)} collective-permute-done((f32[64,128]{1,0:T(8,128)S(1)}, f32[64,128]{1,0:T(8,128)S(1)}, u32[]{:S(2)}, u32[]{:S(2)}) %collective-permute-start.10) | collective-permute-done | bytes 32800 | tf_op jit(solution)/shard_map/ppermute | solution.py:25
  43.3 2.1 %collective-permute-start.11 = (f32[64,128]{1,0:T(8,128)S(1)}, f32[64,128]{1,0:T(8,128)S(1)}, u32[]{:S(2)}, u32[]{:S(2)}) collective-permute-start(f32[64,128]{1,0:T(8,128)S(1)} %add.18), channel_id=1, source_target_pairs={{0,64},{1,65},{2,66},{3,67},{4,68},{5,69},{6,70},{7,71},{8,72},{9,... | collective-permute-start | bytes 98312 | tf_op jit(solution)/shard_map/ppermute | solution.py:25
  45.4 1.9 %collective-permute-done.11 = f32[64,128]{1,0:T(8,128)S(1)} collective-permute-done((f32[64,128]{1,0:T(8,128)S(1)}, f32[64,128]{1,0:T(8,128)S(1)}, u32[]{:S(2)}, u32[]{:S(2)}) %collective-permute-start.11) | collective-permute-done | bytes 32800 | tf_op jit(solution)/shard_map/ppermute | solution.py:25
  47.3 2.5 %collective-permute-start.12 = (f32[64,128]{1,0:T(8,128)S(1)}, f32[64,128]{1,0:T(8,128)S(1)}, u32[]{:S(2)}, u32[]{:S(2)}) collective-permute-start(f32[64,128]{1,0:T(8,128)S(1)} %add.19), channel_id=1, source_target_pairs={{0,128},{1,129},{2,130},{3,131},{4,132},{5,133},{6,134},{7,135},{8... | collective-permute-start | bytes 98312 | tf_op jit(solution)/shard_map/ppermute | solution.py:25
  49.8 2.4 %collective-permute-done.12 = f32[64,128]{1,0:T(8,128)S(1)} collective-permute-done((f32[64,128]{1,0:T(8,128)S(1)}, f32[64,128]{1,0:T(8,128)S(1)}, u32[]{:S(2)}, u32[]{:S(2)}) %collective-permute-start.12) | collective-permute-done | bytes 32800 | tf_op jit(solution)/shard_map/ppermute | solution.py:25
  52.3 0.0 collective-permute-done.6
  52.4 0.1 collective-permute-start.16
  52.5 2.2 %collective-permute-start.15 = (f32[64,128]{1,0:T(8,128)S(1)}, f32[64,128]{1,0:T(8,128)S(1)}, u32[]{:S(2)}, u32[]{:S(2)}) collective-permute-start(f32[64,128]{1,0:T(8,128)S(1)} %add.20), channel_id=1, source_target_pairs={{0,48},{1,49},{2,50},{3,51},{4,52},{5,53},{6,54},{7,55},{8,56},{9,... | collective-permute-start | bytes 98312 | tf_op jit(solution)/shard_map/ppermute | solution.py:25
  54.7 0.9 %collective-permute-start.14 = (f32[64,128]{1,0:T(8,128)S(1)}, f32[64,128]{1,0:T(8,128)S(1)}, u32[]{:S(2)}, u32[]{:S(2)}) collective-permute-start(f32[64,128]{1,0:T(8,128)S(1)} %add.20), channel_id=1, source_target_pairs={{0,32},{1,33},{2,34},{3,35},{4,36},{5,37},{6,38},{7,39},{8,40},{9,... | collective-permute-start | bytes 98312 | tf_op jit(solution)/shard_map/ppermute | solution.py:25
  55.6 1.1 %collective-permute-start.13 = (f32[64,128]{1,0:T(8,128)S(1)}, f32[64,128]{1,0:T(8,128)S(1)}, u32[]{:S(2)}, u32[]{:S(2)}) collective-permute-start(f32[64,128]{1,0:T(8,128)S(1)} %add.20), channel_id=1, source_target_pairs={{0,16},{1,17},{2,18},{3,19},{4,20},{5,21},{6,22},{7,23},{8,24},{9,... | collective-permute-start | bytes 98312 | tf_op jit(solution)/shard_map/ppermute | solution.py:25
  56.7 0.1 pad_add_fusion.place_ref
  56.8 1.0 %collective-permute-done.15 = f32[64,128]{1,0:T(8,128)S(1)} collective-permute-done((f32[64,128]{1,0:T(8,128)S(1)}, f32[64,128]{1,0:T(8,128)S(1)}, u32[]{:S(2)}, u32[]{:S(2)}) %collective-permute-start.15) | collective-permute-done | bytes 32800 | tf_op jit(solution)/shard_map/ppermute | solution.py:25
  57.7 2.7 %collective-permute-done.14 = f32[64,128]{1,0:T(8,128)S(1)} collective-permute-done((f32[64,128]{1,0:T(8,128)S(1)}, f32[64,128]{1,0:T(8,128)S(1)}, u32[]{:S(2)}, u32[]{:S(2)}) %collective-permute-start.14) | collective-permute-done | bytes 32800 | tf_op jit(solution)/shard_map/ppermute | solution.py:25
  60.4 15.3 %shard_map.57 = f32[4096,256]{1,0:T(8,128)} custom-call(s32[2]{0:T(128)S(1)} %pad_add_fusion.place_ref, f32[64,128]{1,0:T(8,128)S(1)} %add_add_fusion.sums_ref, bf16[128,4096]{1,0:T(8,128)(2,1)S(1)} %constant_dynamic-update-slice_fusion.near_ref, bf16[128,4096]{1,0:T(8,128)(2,1)S(1)} %collective-permute-done.16.far_ref, ...), custom_call_target="tpu_custom_call" | custom-call | flops 8589934592 | bytes 4194304 | tf_op jit(solution)/shard_map/pallas_call | solution.py:239
  (16 shorter events, 0.1 us)
Async XLA Ops:
  6.4 11.7 %collective-permute-start.3 = (bf16[8,4096]{1,0:T(8,128)(2,1)}, bf16[8,4096]{1,0:T(8,128)(2,1)S(1)}, u32[]{:S(2)}, u32[]{:S(2)}) collective-permute-start(bf16[8,4096]{1,0:T(8,128)(2,1)} %get-tuple-element.15), channel_id=1, source_target_pairs={{0,192},{1,193},{2,194},{3,195},{4,196},{5,197},{6,198},{7,199},{8... | collective-permute-start | bytes 196616 | tf_op jit(solution)/shard_map/ppermute | solution.py:25
  11.1 7.0 %collective-permute-start.2 = (bf16[8,4096]{1,0:T(8,128)(2,1)}, bf16[8,4096]{1,0:T(8,128)(2,1)S(1)}, u32[]{:S(2)}, u32[]{:S(2)}) collective-permute-start(bf16[8,4096]{1,0:T(8,128)(2,1)} %get-tuple-element.15), channel_id=1, source_target_pairs={{0,128},{1,129},{2,130},{3,131},{4,132},{5,133},{6,134},{7,135},{8... | collective-permute-start | bytes 196616 | tf_op jit(solution)/shard_map/ppermute | solution.py:25
  11.1 7.0 %collective-permute-start.1 = (bf16[8,4096]{1,0:T(8,128)(2,1)}, bf16[8,4096]{1,0:T(8,128)(2,1)S(1)}, u32[]{:S(2)}, u32[]{:S(2)}) collective-permute-start(bf16[8,4096]{1,0:T(8,128)(2,1)} %get-tuple-element.15), channel_id=1, source_target_pairs={{0,64},{1,65},{2,66},{3,67},{4,68},{5,69},{6,70},{7,71},{8,72},{9,... | collective-permute-start | bytes 196616 | tf_op jit(solution)/shard_map/ppermute | solution.py:25
  11.8 13.5 %collective-permute-start = (bf16[512,128]{1,0:T(8,128)(2,1)}, bf16[512,128]{1,0:T(8,128)(2,1)S(1)}, u32[]{:S(2)}, u32[]{:S(2)}) collective-permute-start(bf16[512,128]{1,0:T(8,128)(2,1)} %get-tuple-element.14), channel_id=1, source_target_pairs={{0,4},{1,5},{2,6},{3,7},{4,0},{5,1},{6,2},{7,3},{8,12},{9,13},{10,... | collective-permute-start | bytes 393224 | tf_op jit(solution)/shard_map/ppermute | solution.py:25
  26.1 13.9 %collective-permute-start.9 = (bf16[1024,128]{1,0:T(8,128)(2,1)S(1)}, bf16[1024,128]{1,0:T(8,128)(2,1)S(1)}, u32[]{:S(2)}, u32[]{:S(2)}) collective-permute-start(bf16[1024,128]{1,0:T(8,128)(2,1)S(1)} %pad_maximum_fusion.refs_0_.rest_0_), channel_id=1, source_target_pairs={{0,3},{1,2},{2,1},{3,0},{4,7},{5,6},{6,5},{7,4},{8,11},{9,10},{10,... | collective-permute-start | bytes 786440 | tf_op jit(solution)/shard_map/ppermute | solution.py:25
  26.4 15.0 %collective-permute-start.8 = (bf16[1024,128]{1,0:T(8,128)(2,1)S(1)}, bf16[1024,128]{1,0:T(8,128)(2,1)S(1)}, u32[]{:S(2)}, u32[]{:S(2)}) collective-permute-start(bf16[1024,128]{1,0:T(8,128)(2,1)S(1)} %pad_maximum_fusion.refs_0_.rest_0_), channel_id=1, source_target_pairs={{0,2},{1,3},{2,0},{3,1},{4,6},{5,7},{6,4},{7,5},{8,10},{9,11},{10,... | collective-permute-start | bytes 786440 | tf_op jit(solution)/shard_map/ppermute | solution.py:25
  29.0 12.5 %collective-permute-start.7 = (bf16[1024,128]{1,0:T(8,128)(2,1)S(1)}, bf16[1024,128]{1,0:T(8,128)(2,1)S(1)}, u32[]{:S(2)}, u32[]{:S(2)}) collective-permute-start(bf16[1024,128]{1,0:T(8,128)(2,1)S(1)} %pad_maximum_fusion.refs_0_.rest_0_), channel_id=1, source_target_pairs={{0,1},{1,0},{2,3},{3,2},{4,5},{5,4},{6,7},{7,6},{8,9},{9,8},{10,11... | collective-permute-start | bytes 786440 | tf_op jit(solution)/shard_map/ppermute | solution.py:25
  30.3 22.0 %collective-permute-start.6 = (bf16[32,4096]{1,0:T(8,128)(2,1)S(1)}, bf16[32,4096]{1,0:T(8,128)(2,1)S(1)}, u32[]{:S(2)}, u32[]{:S(2)}) collective-permute-start(bf16[32,4096]{1,0:T(8,128)(2,1)S(1)} %pad_maximum_fusion.1), channel_id=1, source_target_pairs={{0,48},{1,49},{2,50},{3,51},{4,52},{5,53},{6,54},{7,55},{8,56},{9,... | collective-permute-start | bytes 786440 | tf_op jit(solution)/shard_map/ppermute | solution.py:25
  33.1 19.2 %collective-permute-start.5 = (bf16[32,4096]{1,0:T(8,128)(2,1)S(1)}, bf16[32,4096]{1,0:T(8,128)(2,1)S(1)}, u32[]{:S(2)}, u32[]{:S(2)}) collective-permute-start(bf16[32,4096]{1,0:T(8,128)(2,1)S(1)} %pad_maximum_fusion.1), channel_id=1, source_target_pairs={{0,32},{1,33},{2,34},{3,35},{4,36},{5,37},{6,38},{7,39},{8,40},{9,... | collective-permute-start | bytes 786440 | tf_op jit(solution)/shard_map/ppermute | solution.py:25
  40.0 12.3 %collective-permute-start.4 = (bf16[32,4096]{1,0:T(8,128)(2,1)S(1)}, bf16[32,4096]{1,0:T(8,128)(2,1)S(1)}, u32[]{:S(2)}, u32[]{:S(2)}) collective-permute-start(bf16[32,4096]{1,0:T(8,128)(2,1)S(1)} %pad_maximum_fusion.1), channel_id=1, source_target_pairs={{0,16},{1,17},{2,18},{3,19},{4,20},{5,21},{6,22},{7,23},{8,24},{9,... | collective-permute-start | bytes 786440 | tf_op jit(solution)/shard_map/ppermute | solution.py:25
  42.0 1.3 %collective-permute-start.10 = (f32[64,128]{1,0:T(8,128)S(1)}, f32[64,128]{1,0:T(8,128)S(1)}, u32[]{:S(2)}, u32[]{:S(2)}) collective-permute-start(f32[64,128]{1,0:T(8,128)S(1)} %shard_map.56), channel_id=1, source_target_pairs={{0,8},{1,9},{2,10},{3,11},{4,12},{5,13},{6,14},{7,15},{8,0},{9,1},... | collective-permute-start | bytes 98312 | tf_op jit(solution)/shard_map/ppermute | solution.py:25
  43.3 4.0 %collective-permute-start.11 = (f32[64,128]{1,0:T(8,128)S(1)}, f32[64,128]{1,0:T(8,128)S(1)}, u32[]{:S(2)}, u32[]{:S(2)}) collective-permute-start(f32[64,128]{1,0:T(8,128)S(1)} %add.18), channel_id=1, source_target_pairs={{0,64},{1,65},{2,66},{3,67},{4,68},{5,69},{6,70},{7,71},{8,72},{9,... | collective-permute-start | bytes 98312 | tf_op jit(solution)/shard_map/ppermute | solution.py:25
  47.3 5.0 %collective-permute-start.12 = (f32[64,128]{1,0:T(8,128)S(1)}, f32[64,128]{1,0:T(8,128)S(1)}, u32[]{:S(2)}, u32[]{:S(2)}) collective-permute-start(f32[64,128]{1,0:T(8,128)S(1)} %add.19), channel_id=1, source_target_pairs={{0,128},{1,129},{2,130},{3,131},{4,132},{5,133},{6,134},{7,135},{8... | collective-permute-start | bytes 98312 | tf_op jit(solution)/shard_map/ppermute | solution.py:25
  52.4 8.0 %collective-permute-start.16 = (bf16[128,4096]{1,0:T(8,128)(2,1)S(1)}, bf16[128,4096]{1,0:T(8,128)(2,1)S(1)}, u32[]{:S(2)}, u32[]{:S(2)}) collective-permute-start(bf16[128,4096]{1,0:T(8,128)(2,1)S(1)} %constant_dynamic-update-slice_fusion.near_ref), channel_id=1, source_target_pairs={{0,8},{1,9},{2,10},{3,11},{4,12},{5,13},{6,14},{7,15},{8,0},{9,1},... | collective-permute-start | bytes 3145736 | tf_op jit(solution)/shard_map/ppermute | solution.py:25
  52.5 5.2 %collective-permute-start.15 = (f32[64,128]{1,0:T(8,128)S(1)}, f32[64,128]{1,0:T(8,128)S(1)}, u32[]{:S(2)}, u32[]{:S(2)}) collective-permute-start(f32[64,128]{1,0:T(8,128)S(1)} %add.20), channel_id=1, source_target_pairs={{0,48},{1,49},{2,50},{3,51},{4,52},{5,53},{6,54},{7,55},{8,56},{9,... | collective-permute-start | bytes 98312 | tf_op jit(solution)/shard_map/ppermute | solution.py:25
  54.7 5.7 %collective-permute-start.14 = (f32[64,128]{1,0:T(8,128)S(1)}, f32[64,128]{1,0:T(8,128)S(1)}, u32[]{:S(2)}, u32[]{:S(2)}) collective-permute-start(f32[64,128]{1,0:T(8,128)S(1)} %add.20), channel_id=1, source_target_pairs={{0,32},{1,33},{2,34},{3,35},{4,36},{5,37},{6,38},{7,39},{8,40},{9,... | collective-permute-start | bytes 98312 | tf_op jit(solution)/shard_map/ppermute | solution.py:25
  55.6 4.8 %collective-permute-start.13 = (f32[64,128]{1,0:T(8,128)S(1)}, f32[64,128]{1,0:T(8,128)S(1)}, u32[]{:S(2)}, u32[]{:S(2)}) collective-permute-start(f32[64,128]{1,0:T(8,128)S(1)} %add.20), channel_id=1, source_target_pairs={{0,16},{1,17},{2,18},{3,19},{4,20},{5,21},{6,22},{7,23},{8,24},{9,... | collective-permute-start | bytes 98312 | tf_op jit(solution)/shard_map/ppermute | solution.py:25

commit v3 on v2

--- a/solution.py
+++ b/solution.py
@@ -34,8 +34,7 @@
     return lax.ppermute(array, BOTH, pairs)
 
 
-def sides_kernel(lengths_ref, inputs_ref, cotangents_ref, maps_ref, queries_ref, sides_ref, passed_ref,
-                 read_in, read_out, maps, sem):
+def sides_kernel(lengths_ref, inputs_ref, cotangents_ref, maps_ref, sides_ref, read_in, read_out, maps, sem):
     rank = maps_ref.shape[1] // 2
     sequences = lengths_ref.shape[0]
     slots = inputs_ref.shape[0] // sequences
@@ -48,8 +47,6 @@
         copies.append(pltpu.make_async_copy(cotangents_ref.at[rows], read_out.at[rows], sem.at[2 * s + 1]))
     for copy in copies:
         copy.start()
-    last = pltpu.make_async_copy(queries_ref, passed_ref, sem.at[2 * sequences + 1])
-    last.start()
     first.wait()
     row = lax.broadcasted_iota(jnp.int32, (slots, 2 * rank), 0)
     lane = lax.broadcasted_iota(jnp.int32, (slots, 2 * rank), 1)
@@ -61,33 +58,29 @@
         of_out = jnp.dot(read_out[rows], maps[...], preferred_element_type=F32)
         sides = jnp.where(row < lengths_ref[s], jnp.where(lane < rank, of_in, of_out), 0.0)
         sides_ref[rows] = sides.astype(BF16)
-    last.wait()
-
-
-def sides_of(inputs, cotangents, sketch_maps, lengths, queries):
+
+
+def sides_of(inputs, cotangents, sketch_maps, lengths):
     rows, width = inputs.shape
     both = sketch_maps.shape[1]
     sequences = lengths.shape[0]
     anywhere = pl.BlockSpec(memory_space=pl.ANY)
     return pl.pallas_call(
         sides_kernel,
-        in_specs=[pl.BlockSpec(memory_space=pltpu.SMEM)] + [anywhere] * 4,
-        out_specs=[pl.BlockSpec(memory_space=pltpu.VMEM)] * 2,
+        in_specs=[pl.BlockSpec(memory_space=pltpu.SMEM)] + [anywhere] * 3,
+        out_specs=pl.BlockSpec(memory_space=pltpu.VMEM),
         scratch_shapes=[
             pltpu.VMEM((rows, width), BF16),
             pltpu.VMEM((rows, width), BF16),
             pltpu.VMEM((width, both), BF16),
-            pltpu.SemaphoreType.DMA((2 * sequences + 2,)),
+            pltpu.SemaphoreType.DMA((2 * sequences + 1,)),
         ],
-        out_shape=[
-            jax.ShapeDtypeStruct((rows, both), BF16),
-            jax.ShapeDtypeStruct(queries.shape, BF16),
-        ],
+        out_shape=jax.ShapeDtypeStruct((rows, both), BF16),
         compiler_params=pltpu.CompilerParams(vmem_limit_bytes=56 * MIB),
         cost_estimate=pl.CostEstimate(
             flops=4 * rows * width * both, bytes_accessed=4 * rows * width, transcendentals=0
         ),
-    )(lengths, inputs, cotangents, sketch_maps, queries)
+    )(lengths, inputs, cotangents, sketch_maps)
 
 
 def moments_kernel(*refs):
@@ -261,10 +254,10 @@
 
 
 def shards(inputs, cotangents, sketch_maps, lengths, queries):
-    sides, queries = sides_of(inputs, cotangents, sketch_maps, lengths, queries)
+    line = jnp.concatenate([queries] + [exchange(queries, 8 * d, 0) for d in (1, 2, 3)])
+    sides = sides_of(inputs, cotangents, sketch_maps, lengths)
+    sides, line = lax.optimization_barrier((sides, line))
     pair = jnp.concatenate([sides, exchange(sides, 0, 4)])
-    line = jnp.concatenate([queries] + [exchange(queries, 8 * d, 0) for d in (1, 2, 3)])
-    pair, line = lax.optimization_barrier((pair, line))
     parts = [pair] + [exchange(pair, 0, d) for d in (1, 2, 3)]
     lines = [line] + [exchange(line, 2 * d, 0) for d in (1, 2, 3)]
     sums = moments_of(parts)

time: 76 us -> 70.7 us (0.930)
  starting transfers between devices: 29.9 us -> 27 us
  other arithmetic: 1.88 us -> 0.12 us
  waiting for transfers between devices: 21.6 us -> 20 us
  local copies, waits for them, and re-layouts: 0.08 us -> 1.05 us
    ppermute x17, starting transfers between devices: 29.9 us -> 27 us  [exchange(): return lax.ppermute(array, BOTH, pairs)]
    ppermute x17, waiting for transfers between devices: 21.6 us -> 20 us  [exchange(): return lax.ppermute(array, BOTH, pairs)]
    unnamed x3 -> x6, local copies, waits for them, and re-layouts: 0.06 us -> 1.01 us
    concatenate x1 -> x0, other arithmetic: 0.92 us -> none  [shards(): pair = jnp.concatenate([sides, exchange(sides, 0, 4)])]
    concatenate x1, other arithmetic: 0.86 us -> 0.02 us  [shards(): jnp.concatenate([queries] + [exchange(queries, 8 * d, 0) for d in (1, 2,...]
  transfers between devices with their start and end apart: 17 -> 17, of which waited for: 7 -> 7; matrix products, arithmetic and copies ran while one was open for 1% -> 1% of each run, Pallas kernels for 1% -> 10%
where the time goes in v3:
time: 70.7 us; the launch traced here: 70.6 us
  starting transfers between devices  27 us (38%)
  Pallas kernels  22.1 us (31%)
  waiting for transfers between devices  20 us (28%)
  local copies, waits for them, and re-layouts  1.05 us (1%)
    ppermute x17, starting transfers between devices, exchange(): return lax.ppermute(array, BOTH, pairs)  27 us
    ppermute x17, waiting for transfers between devices, exchange(): return lax.ppermute(array, BOTH, pairs)  20 us
    pallas_call x1, Pallas kernels, scores_of(): pl.pallas_call(functools.partial(scores_kernel, tile=tile, together=toget...  15.3 us
    pallas_call x1, Pallas kernels, sides_of(): pl.pallas_call(sides_kernel, in_specs=[pl.BlockSpec(memory_space=pltpu.SM...  6.34 us
  transfers between devices with their start and end apart: 17, of which 7 were waited for; matrix products, arithmetic and copies ran while one was open for 1% of the time, Pallas kernels for 10%

profile of v3, /device:TPU:24, one launch (start us, length us, event | category | flops | bytes accessed | tf_op | source)
XLA Modules:
  0.0 70.6 jit_solution(3057379487821662556)
XLA Ops:
  0.0 3.3 %collective-permute-start.1 = (bf16[8,4096]{1,0:T(8,128)(2,1)}, bf16[8,4096]{1,0:T(8,128)(2,1)S(1)}, u32[]{:S(2)}, u32[]{:S(2)}) collective-permute-start(bf16[8,4096]{1,0:T(8,128)(2,1)} %param.9), channel_id=1, source_target_pairs={{0,128},{1,129},{2,130},{3,131},{4,132},{5,133},{6,134},{7,135},{8... | collective-permute-start | bytes 196616 | tf_op jit(solution)/shard_map/ppermute | solution.py:25
  3.3 1.9 %collective-permute-start = (bf16[8,4096]{1,0:T(8,128)(2,1)}, bf16[8,4096]{1,0:T(8,128)(2,1)S(1)}, u32[]{:S(2)}, u32[]{:S(2)}) collective-permute-start(bf16[8,4096]{1,0:T(8,128)(2,1)} %param.9), channel_id=1, source_target_pairs={{0,64},{1,65},{2,66},{3,67},{4,68},{5,69},{6,70},{7,71},{8,72},{9,... | collective-permute-start | bytes 196616 | tf_op jit(solution)/shard_map/ppermute | solution.py:25
  5.2 0.0 collective-permute-start.2
  5.2 6.3 %shard_map.55 = bf16[512,128]{1,0:T(8,128)(2,1)} custom-call(s32[4]{0:T(128)} %lengths_ref.1, bf16[512,4096]{1,0:T(8,128)(2,1)} %inputs_ref.1, bf16[512,4096]{1,0:T(8,128)(2,1)} %cotangents_ref.1, bf16[4096,128]{1,0:T(8,128)(2,1)} %maps_ref.1), custom_call_target="tpu_custom_call" | custom-call | flops 1073741824 | bytes 8388608 | tf_op jit(solution)/shard_map/pallas_call | solution.py:68
  11.5 0.0 collective-permute-done.1
  11.6 0.0 collective-permute-done
  11.6 6.5 %collective-permute-start.6 = (bf16[512,128]{1,0:T(8,128)(2,1)}, bf16[512,128]{1,0:T(8,128)(2,1)S(1)}, u32[]{:S(2)}, u32[]{:S(2)}) collective-permute-start(bf16[512,128]{1,0:T(8,128)(2,1)} %shard_map.55), channel_id=1, source_target_pairs={{0,4},{1,5},{2,6},{3,7},{4,0},{5,1},{6,2},{7,3},{8,12},{9,13},{10,... | collective-permute-start | bytes 393224 | tf_op jit(solution)/shard_map/ppermute | solution.py:25
  18.1 0.9 %constant_dynamic-update-slice_fusion.1 = bf16[1024,128]{1,0:T(8,128)(2,1)S(1)} fusion(bf16[512,128]{1,0:T(8,128)(2,1)} %shard_map.55), kind=kLoop, calls=%fused_computation.3 | loop fusion | bytes 262144
  19.0 3.0 %collective-permute-done.6 = bf16[512,128]{1,0:T(8,128)(2,1)S(1)} collective-permute-done((bf16[512,128]{1,0:T(8,128)(2,1)}, bf16[512,128]{1,0:T(8,128)(2,1)S(1)}, u32[]{:S(2)}, u32[]{:S(2)}) %collective-permute-start.6) | collective-permute-done | bytes 131104 | tf_op jit(solution)/shard_map/ppermute | solution.py:25
  22.1 1.4 %collective-permute-start.9 = (bf16[1024,128]{1,0:T(8,128)(2,1)S(1)}, bf16[1024,128]{1,0:T(8,128)(2,1)S(1)}, u32[]{:S(2)}, u32[]{:S(2)}) collective-permute-start(bf16[1024,128]{1,0:T(8,128)(2,1)S(1)} %constant_dynamic-update-slice_fusion.refs_0_.rest_0_), channel_id=1, source_target_pairs={{0,3},{1,2},{2,1},{3,0},{4,7},{5,6},{6,5},{7,4},{8,11},{9,10},{10,... | collective-permute-start | bytes 786440 | tf_op jit(solution)/shard_map/ppermute | solution.py:25
  23.5 1.5 %collective-permute-start.8 = (bf16[1024,128]{1,0:T(8,128)(2,1)S(1)}, bf16[1024,128]{1,0:T(8,128)(2,1)S(1)}, u32[]{:S(2)}, u32[]{:S(2)}) collective-permute-start(bf16[1024,128]{1,0:T(8,128)(2,1)S(1)} %constant_dynamic-update-slice_fusion.refs_0_.rest_0_), channel_id=1, source_target_pairs={{0,2},{1,3},{2,0},{3,1},{4,6},{5,7},{6,4},{7,5},{8,10},{9,11},{10,... | collective-permute-start | bytes 786440 | tf_op jit(solution)/shard_map/ppermute | solution.py:25
  25.0 1.3 %collective-permute-start.7 = (bf16[1024,128]{1,0:T(8,128)(2,1)S(1)}, bf16[1024,128]{1,0:T(8,128)(2,1)S(1)}, u32[]{:S(2)}, u32[]{:S(2)}) collective-permute-start(bf16[1024,128]{1,0:T(8,128)(2,1)S(1)} %constant_dynamic-update-slice_fusion.refs_0_.rest_0_), channel_id=1, source_target_pairs={{0,1},{1,0},{2,3},{3,2},{4,5},{5,4},{6,7},{7,6},{8,9},{9,8},{10,11... | collective-permute-start | bytes 786440 | tf_op jit(solution)/shard_map/ppermute | solution.py:25
  26.3 2.8 %collective-permute-start.5 = (bf16[32,4096]{1,0:T(8,128)(2,1)S(1)}, bf16[32,4096]{1,0:T(8,128)(2,1)S(1)}, u32[]{:S(2)}, u32[]{:S(2)}) collective-permute-start(bf16[32,4096]{1,0:T(8,128)(2,1)S(1)} %pad_maximum_fusion), channel_id=1, source_target_pairs={{0,48},{1,49},{2,50},{3,51},{4,52},{5,53},{6,54},{7,55},{8,56},{9,... | collective-permute-start | bytes 786440 | tf_op jit(solution)/shard_map/ppermute | solution.py:25
  29.0 0.8 %collective-permute-start.4 = (bf16[32,4096]{1,0:T(8,128)(2,1)S(1)}, bf16[32,4096]{1,0:T(8,128)(2,1)S(1)}, u32[]{:S(2)}, u32[]{:S(2)}) collective-permute-start(bf16[32,4096]{1,0:T(8,128)(2,1)S(1)} %pad_maximum_fusion), channel_id=1, source_target_pairs={{0,32},{1,33},{2,34},{3,35},{4,36},{5,37},{6,38},{7,39},{8,40},{9,... | collective-permute-start | bytes 786440 | tf_op jit(solution)/shard_map/ppermute | solution.py:25
  29.8 4.8 %collective-permute-done.9.refs_3_.rest_3_ = bf16[1024,128]{1,0:T(8,128)(2,1)S(1)} collective-permute-done((bf16[1024,128]{1,0:T(8,128)(2,1)S(1)}, bf16[1024,128]{1,0:T(8,128)(2,1)S(1)}, u32[]{:S(2)}, u32[]{:S(2)}) %collective-permute-start.9) | collective-permute-done | bytes 262176 | tf_op jit(solution)/shard_map/ppermute | solution.py:25
  34.6 1.5 %collective-permute-start.3 = (bf16[32,4096]{1,0:T(8,128)(2,1)S(1)}, bf16[32,4096]{1,0:T(8,128)(2,1)S(1)}, u32[]{:S(2)}, u32[]{:S(2)}) collective-permute-start(bf16[32,4096]{1,0:T(8,128)(2,1)S(1)} %pad_maximum_fusion), channel_id=1, source_target_pairs={{0,16},{1,17},{2,18},{3,19},{4,20},{5,21},{6,22},{7,23},{8,24},{9,... | collective-permute-start | bytes 786440 | tf_op jit(solution)/shard_map/ppermute | solution.py:25
  36.1 0.5 shard_map.56
  36.6 0.1 collective-permute-start.10
  36.7 1.2 %collective-permute-done.10 = f32[64,128]{1,0:T(8,128)S(1)} collective-permute-done((f32[64,128]{1,0:T(8,128)S(1)}, f32[64,128]{1,0:T(8,128)S(1)}, u32[]{:S(2)}, u32[]{:S(2)}) %collective-permute-start.10) | collective-permute-done | bytes 32800 | tf_op jit(solution)/shard_map/ppermute | solution.py:25
  37.9 0.1 collective-permute-start.11
  38.0 3.8 %collective-permute-done.11 = f32[64,128]{1,0:T(8,128)S(1)} collective-permute-done((f32[64,128]{1,0:T(8,128)S(1)}, f32[64,128]{1,0:T(8,128)S(1)}, u32[]{:S(2)}, u32[]{:S(2)}) %collective-permute-start.11) | collective-permute-done | bytes 32800 | tf_op jit(solution)/shard_map/ppermute | solution.py:25
  41.8 1.6 %collective-permute-start.12 = (f32[64,128]{1,0:T(8,128)S(1)}, f32[64,128]{1,0:T(8,128)S(1)}, u32[]{:S(2)}, u32[]{:S(2)}) collective-permute-start(f32[64,128]{1,0:T(8,128)S(1)} %add.19), channel_id=1, source_target_pairs={{0,128},{1,129},{2,130},{3,131},{4,132},{5,133},{6,134},{7,135},{8... | collective-permute-start | bytes 98312 | tf_op jit(solution)/shard_map/ppermute | solution.py:25
  43.5 3.5 %collective-permute-done.12 = f32[64,128]{1,0:T(8,128)S(1)} collective-permute-done((f32[64,128]{1,0:T(8,128)S(1)}, f32[64,128]{1,0:T(8,128)S(1)}, u32[]{:S(2)}, u32[]{:S(2)}) %collective-permute-start.12) | collective-permute-done | bytes 32800 | tf_op jit(solution)/shard_map/ppermute | solution.py:25
  47.1 0.1 collective-permute-start.16
  47.2 2.2 %collective-permute-start.15 = (f32[64,128]{1,0:T(8,128)S(1)}, f32[64,128]{1,0:T(8,128)S(1)}, u32[]{:S(2)}, u32[]{:S(2)}) collective-permute-start(f32[64,128]{1,0:T(8,128)S(1)} %add.20), channel_id=1, source_target_pairs={{0,48},{1,49},{2,50},{3,51},{4,52},{5,53},{6,54},{7,55},{8,56},{9,... | collective-permute-start | bytes 98312 | tf_op jit(solution)/shard_map/ppermute | solution.py:25
  49.4 0.9 %collective-permute-start.14 = (f32[64,128]{1,0:T(8,128)S(1)}, f32[64,128]{1,0:T(8,128)S(1)}, u32[]{:S(2)}, u32[]{:S(2)}) collective-permute-start(f32[64,128]{1,0:T(8,128)S(1)} %add.20), channel_id=1, source_target_pairs={{0,32},{1,33},{2,34},{3,35},{4,36},{5,37},{6,38},{7,39},{8,40},{9,... | collective-permute-start | bytes 98312 | tf_op jit(solution)/shard_map/ppermute | solution.py:25
  50.3 1.1 %collective-permute-start.13 = (f32[64,128]{1,0:T(8,128)S(1)}, f32[64,128]{1,0:T(8,128)S(1)}, u32[]{:S(2)}, u32[]{:S(2)}) collective-permute-start(f32[64,128]{1,0:T(8,128)S(1)} %add.20), channel_id=1, source_target_pairs={{0,16},{1,17},{2,18},{3,19},{4,20},{5,21},{6,22},{7,23},{8,24},{9,... | collective-permute-start | bytes 98312 | tf_op jit(solution)/shard_map/ppermute | solution.py:25
  51.4 0.1 pad_add_fusion.place_ref
  51.5 1.0 %collective-permute-done.15 = f32[64,128]{1,0:T(8,128)S(1)} collective-permute-done((f32[64,128]{1,0:T(8,128)S(1)}, f32[64,128]{1,0:T(8,128)S(1)}, u32[]{:S(2)}, u32[]{:S(2)}) %collective-permute-start.15) | collective-permute-done | bytes 32800 | tf_op jit(solution)/shard_map/ppermute | solution.py:25
  52.5 2.6 %collective-permute-done.14 = f32[64,128]{1,0:T(8,128)S(1)} collective-permute-done((f32[64,128]{1,0:T(8,128)S(1)}, f32[64,128]{1,0:T(8,128)S(1)}, u32[]{:S(2)}, u32[]{:S(2)}) %collective-permute-start.14) | collective-permute-done | bytes 32800 | tf_op jit(solution)/shard_map/ppermute | solution.py:25
  55.1 0.0 collective-permute-done.16.far_ref
  55.1 15.3 %shard_map.57 = f32[4096,256]{1,0:T(8,128)} custom-call(s32[2]{0:T(128)S(1)} %pad_add_fusion.place_ref, f32[64,128]{1,0:T(8,128)S(1)} %add_add_fusion.sums_ref, bf16[128,4096]{1,0:T(8,128)(2,1)S(1)} %constant_dynamic-update-slice_fusion.2.near_ref, bf16[128,4096]{1,0:T(8,128)(2,1)S(1)} %collective-permute-done.16.far_ref, ...), custom_call_target="tpu_custom_call" | custom-call | flops 8589934592 | bytes 4194304 | tf_op jit(solution)/shard_map/pallas_call | solution.py:232
  (19 shorter events, 0.2 us)
Async XLA Ops:
  0.0 11.6 %copy-start = (bf16[8,4096]{1,0:T(8,128)(2,1)S(1)}, bf16[8,4096]{1,0:T(8,128)(2,1)}, u32[]{:S(2)}) copy-start(bf16[8,4096]{1,0:T(8,128)(2,1)} %param.9) | copy-start | bytes 196612
  0.0 11.5 %collective-permute-start.1 = (bf16[8,4096]{1,0:T(8,128)(2,1)}, bf16[8,4096]{1,0:T(8,128)(2,1)S(1)}, u32[]{:S(2)}, u32[]{:S(2)}) collective-permute-start(bf16[8,4096]{1,0:T(8,128)(2,1)} %param.9), channel_id=1, source_target_pairs={{0,128},{1,129},{2,130},{3,131},{4,132},{5,133},{6,134},{7,135},{8... | collective-permute-start | bytes 196616 | tf_op jit(solution)/shard_map/ppermute | solution.py:25
  3.3 8.3 %collective-permute-start = (bf16[8,4096]{1,0:T(8,128)(2,1)}, bf16[8,4096]{1,0:T(8,128)(2,1)S(1)}, u32[]{:S(2)}, u32[]{:S(2)}) collective-permute-start(bf16[8,4096]{1,0:T(8,128)(2,1)} %param.9), channel_id=1, source_target_pairs={{0,64},{1,65},{2,66},{3,67},{4,68},{5,69},{6,70},{7,71},{8,72},{9,... | collective-permute-start | bytes 196616 | tf_op jit(solution)/shard_map/ppermute | solution.py:25
  5.2 6.4 %collective-permute-start.2 = (bf16[8,4096]{1,0:T(8,128)(2,1)}, bf16[8,4096]{1,0:T(8,128)(2,1)S(1)}, u32[]{:S(2)}, u32[]{:S(2)}) collective-permute-start(bf16[8,4096]{1,0:T(8,128)(2,1)} %param.9), channel_id=1, source_target_pairs={{0,192},{1,193},{2,194},{3,195},{4,196},{5,197},{6,198},{7,199},{8... | collective-permute-start | bytes 196616 | tf_op jit(solution)/shard_map/ppermute | solution.py:25
  11.6 10.5 %collective-permute-start.6 = (bf16[512,128]{1,0:T(8,128)(2,1)}, bf16[512,128]{1,0:T(8,128)(2,1)S(1)}, u32[]{:S(2)}, u32[]{:S(2)}) collective-permute-start(bf16[512,128]{1,0:T(8,128)(2,1)} %shard_map.55), channel_id=1, source_target_pairs={{0,4},{1,5},{2,6},{3,7},{4,0},{5,1},{6,2},{7,3},{8,12},{9,13},{10,... | collective-permute-start | bytes 393224 | tf_op jit(solution)/shard_map/ppermute | solution.py:25
  22.1 12.5 %collective-permute-start.9 = (bf16[1024,128]{1,0:T(8,128)(2,1)S(1)}, bf16[1024,128]{1,0:T(8,128)(2,1)S(1)}, u32[]{:S(2)}, u32[]{:S(2)}) collective-permute-start(bf16[1024,128]{1,0:T(8,128)(2,1)S(1)} %constant_dynamic-update-slice_fusion.refs_0_.rest_0_), channel_id=1, source_target_pairs={{0,3},{1,2},{2,1},{3,0},{4,7},{5,6},{6,5},{7,4},{8,11},{9,10},{10,... | collective-permute-start | bytes 786440 | tf_op jit(solution)/shard_map/ppermute | solution.py:25
  23.5 12.6 %collective-permute-start.8 = (bf16[1024,128]{1,0:T(8,128)(2,1)S(1)}, bf16[1024,128]{1,0:T(8,128)(2,1)S(1)}, u32[]{:S(2)}, u32[]{:S(2)}) collective-permute-start(bf16[1024,128]{1,0:T(8,128)(2,1)S(1)} %constant_dynamic-update-slice_fusion.refs_0_.rest_0_), channel_id=1, source_target_pairs={{0,2},{1,3},{2,0},{3,1},{4,6},{5,7},{6,4},{7,5},{8,10},{9,11},{10,... | collective-permute-start | bytes 786440 | tf_op jit(solution)/shard_map/ppermute | solution.py:25
  25.0 11.1 %collective-permute-start.7 = (bf16[1024,128]{1,0:T(8,128)(2,1)S(1)}, bf16[1024,128]{1,0:T(8,128)(2,1)S(1)}, u32[]{:S(2)}, u32[]{:S(2)}) collective-permute-start(bf16[1024,128]{1,0:T(8,128)(2,1)S(1)} %constant_dynamic-update-slice_fusion.refs_0_.rest_0_), channel_id=1, source_target_pairs={{0,1},{1,0},{2,3},{3,2},{4,5},{5,4},{6,7},{7,6},{8,9},{9,8},{10,11... | collective-permute-start | bytes 786440 | tf_op jit(solution)/shard_map/ppermute | solution.py:25
  26.3 20.7 %collective-permute-start.5 = (bf16[32,4096]{1,0:T(8,128)(2,1)S(1)}, bf16[32,4096]{1,0:T(8,128)(2,1)S(1)}, u32[]{:S(2)}, u32[]{:S(2)}) collective-permute-start(bf16[32,4096]{1,0:T(8,128)(2,1)S(1)} %pad_maximum_fusion), channel_id=1, source_target_pairs={{0,48},{1,49},{2,50},{3,51},{4,52},{5,53},{6,54},{7,55},{8,56},{9,... | collective-permute-start | bytes 786440 | tf_op jit(solution)/shard_map/ppermute | solution.py:25
  29.0 18.0 %collective-permute-start.4 = (bf16[32,4096]{1,0:T(8,128)(2,1)S(1)}, bf16[32,4096]{1,0:T(8,128)(2,1)S(1)}, u32[]{:S(2)}, u32[]{:S(2)}) collective-permute-start(bf16[32,4096]{1,0:T(8,128)(2,1)S(1)} %pad_maximum_fusion), channel_id=1, source_target_pairs={{0,32},{1,33},{2,34},{3,35},{4,36},{5,37},{6,38},{7,39},{8,40},{9,... | collective-permute-start | bytes 786440 | tf_op jit(solution)/shard_map/ppermute | solution.py:25
  34.6 12.4 %collective-permute-start.3 = (bf16[32,4096]{1,0:T(8,128)(2,1)S(1)}, bf16[32,4096]{1,0:T(8,128)(2,1)S(1)}, u32[]{:S(2)}, u32[]{:S(2)}) collective-permute-start(bf16[32,4096]{1,0:T(8,128)(2,1)S(1)} %pad_maximum_fusion), channel_id=1, source_target_pairs={{0,16},{1,17},{2,18},{3,19},{4,20},{5,21},{6,22},{7,23},{8,24},{9,... | collective-permute-start | bytes 786440 | tf_op jit(solution)/shard_map/ppermute | solution.py:25
  36.6 1.3 %collective-permute-start.10 = (f32[64,128]{1,0:T(8,128)S(1)}, f32[64,128]{1,0:T(8,128)S(1)}, u32[]{:S(2)}, u32[]{:S(2)}) collective-permute-start(f32[64,128]{1,0:T(8,128)S(1)} %shard_map.56), channel_id=1, source_target_pairs={{0,8},{1,9},{2,10},{3,11},{4,12},{5,13},{6,14},{7,15},{8,0},{9,1},... | collective-permute-start | bytes 98312 | tf_op jit(solution)/shard_map/ppermute | solution.py:25
  37.9 3.9 %collective-permute-start.11 = (f32[64,128]{1,0:T(8,128)S(1)}, f32[64,128]{1,0:T(8,128)S(1)}, u32[]{:S(2)}, u32[]{:S(2)}) collective-permute-start(f32[64,128]{1,0:T(8,128)S(1)} %add.18), channel_id=1, source_target_pairs={{0,64},{1,65},{2,66},{3,67},{4,68},{5,69},{6,70},{7,71},{8,72},{9,... | collective-permute-start | bytes 98312 | tf_op jit(solution)/shard_map/ppermute | solution.py:25
  41.8 5.2 %collective-permute-start.12 = (f32[64,128]{1,0:T(8,128)S(1)}, f32[64,128]{1,0:T(8,128)S(1)}, u32[]{:S(2)}, u32[]{:S(2)}) collective-permute-start(f32[64,128]{1,0:T(8,128)S(1)} %add.19), channel_id=1, source_target_pairs={{0,128},{1,129},{2,130},{3,131},{4,132},{5,133},{6,134},{7,135},{8... | collective-permute-start | bytes 98312 | tf_op jit(solution)/shard_map/ppermute | solution.py:25
  47.1 8.0 %collective-permute-start.16 = (bf16[128,4096]{1,0:T(8,128)(2,1)S(1)}, bf16[128,4096]{1,0:T(8,128)(2,1)S(1)}, u32[]{:S(2)}, u32[]{:S(2)}) collective-permute-start(bf16[128,4096]{1,0:T(8,128)(2,1)S(1)} %constant_dynamic-update-slice_fusion.2.near_ref), channel_id=1, source_target_pairs={{0,8},{1,9},{2,10},{3,11},{4,12},{5,13},{6,14},{7,15},{8,0},{9,1},... | collective-permute-start | bytes 3145736 | tf_op jit(solution)/shard_map/ppermute | solution.py:25
  47.2 5.2 %collective-permute-start.15 = (f32[64,128]{1,0:T(8,128)S(1)}, f32[64,128]{1,0:T(8,128)S(1)}, u32[]{:S(2)}, u32[]{:S(2)}) collective-permute-start(f32[64,128]{1,0:T(8,128)S(1)} %add.20), channel_id=1, source_target_pairs={{0,48},{1,49},{2,50},{3,51},{4,52},{5,53},{6,54},{7,55},{8,56},{9,... | collective-permute-start | bytes 98312 | tf_op jit(solution)/shard_map/ppermute | solution.py:25
  49.4 5.7 %collective-permute-start.14 = (f32[64,128]{1,0:T(8,128)S(1)}, f32[64,128]{1,0:T(8,128)S(1)}, u32[]{:S(2)}, u32[]{:S(2)}) collective-permute-start(f32[64,128]{1,0:T(8,128)S(1)} %add.20), channel_id=1, source_target_pairs={{0,32},{1,33},{2,34},{3,35},{4,36},{5,37},{6,38},{7,39},{8,40},{9,... | collective-permute-start | bytes 98312 | tf_op jit(solution)/shard_map/ppermute | solution.py:25
  50.3 4.8 %collective-permute-start.13 = (f32[64,128]{1,0:T(8,128)S(1)}, f32[64,128]{1,0:T(8,128)S(1)}, u32[]{:S(2)}, u32[]{:S(2)}) collective-permute-start(f32[64,128]{1,0:T(8,128)S(1)} %add.20), channel_id=1, source_target_pairs={{0,16},{1,17},{2,18},{3,19},{4,20},{5,21},{6,22},{7,23},{8,24},{9,... | collective-permute-start | bytes 98312 | tf_op jit(solution)/shard_map/ppermute | solution.py:25

commit v4 on v3

--- a/solution.py
+++ b/solution.py
@@ -34,7 +34,7 @@
     return lax.ppermute(array, BOTH, pairs)
 
 
-def sides_kernel(lengths_ref, inputs_ref, cotangents_ref, maps_ref, sides_ref, read_in, read_out, maps, sem):
+def sides_kernel(lengths_ref, inputs_ref, cotangents_ref, maps_ref, sides_ref, read_in, read_out, maps, sem, ahead=3):
     rank = maps_ref.shape[1] // 2
     sequences = lengths_ref.shape[0]
     slots = inputs_ref.shape[0] // sequences
@@ -45,7 +45,7 @@
         rows = pl.ds(s * slots, slots)
         copies.append(pltpu.make_async_copy(inputs_ref.at[rows], read_in.at[rows], sem.at[2 * s]))
         copies.append(pltpu.make_async_copy(cotangents_ref.at[rows], read_out.at[rows], sem.at[2 * s + 1]))
-    for copy in copies:
+    for copy in copies[: 2 * ahead]:
         copy.start()
     first.wait()
     row = lax.broadcasted_iota(jnp.int32, (slots, 2 * rank), 0)
@@ -53,8 +53,10 @@
     for s in range(sequences):
         rows = pl.ds(s * slots, slots)
         copies[2 * s].wait()
+        copies[2 * s + 1].wait()
+        for copy in copies[2 * (s + ahead) : 2 * (s + ahead + 1)]:
+            copy.start()
         of_in = jnp.dot(read_in[rows], maps[...], preferred_element_type=F32)
-        copies[2 * s + 1].wait()
         of_out = jnp.dot(read_out[rows], maps[...], preferred_element_type=F32)
         sides = jnp.where(row < lengths_ref[s], jnp.where(lane < rank, of_in, of_out), 0.0)
         sides_ref[rows] = sides.astype(BF16)
@@ -214,9 +216,8 @@
                 written(round_ - 2, h).wait()
 
         for h in range(together):
+            build(jnp.minimum(round_ * together + h + 1, tiles - 1), sketches[(h + 1) % 2])
             ready[(round_ % 2) * together + h] = score(sketches[h % 2], moved[h % 2])
-            build(jnp.minimum(round_ * together + h + 1, tiles - 1), sketches[(h + 1) % 2])
-        for h in range(together):
             written(round_, h).start()
 
     for round_ in (rounds - 2, rounds - 1):

time: 70.7 us -> 70.2 us (level)
  transfers between devices with their start and end apart: 17 -> 17, of which waited for: 7 -> 8; matrix products, arithmetic and copies ran while one was open for 1% -> 1% of each run, Pallas kernels for 10% -> 9%
where the time goes in v4:
time: 70.2 us; the launch traced here: 70 us
  starting transfers between devices  26.8 us (38%)
  Pallas kernels  21.6 us (31%)
  waiting for transfers between devices  20.2 us (29%)
  local copies, waits for them, and re-layouts  1.05 us (1%)
    ppermute x17, starting transfers between devices, exchange(): return lax.ppermute(array, BOTH, pairs)  26.8 us
    ppermute x17, waiting for transfers between devices, exchange(): return lax.ppermute(array, BOTH, pairs)  20.2 us
    pallas_call x1, Pallas kernels, scores_of(): pl.pallas_call(functools.partial(scores_kernel, tile=tile, together=toget...  15 us
    pallas_call x1, Pallas kernels, sides_of(): pl.pallas_call(sides_kernel, in_specs=[pl.BlockSpec(memory_space=pltpu.SM...  6.06 us
  transfers between devices with their start and end apart: 17, of which 8 were waited for; matrix products, arithmetic and copies ran while one was open for 1% of the time, Pallas kernels for 9%

profile of v4, /device:TPU:24, one launch (start us, length us, event | category | flops | bytes accessed | tf_op | source)
XLA Modules:
  0.0 70.0 jit_solution(16183628153813622913)
XLA Ops:
  0.0 3.3 %collective-permute-start.1 = (bf16[8,4096]{1,0:T(8,128)(2,1)}, bf16[8,4096]{1,0:T(8,128)(2,1)S(1)}, u32[]{:S(2)}, u32[]{:S(2)}) collective-permute-start(bf16[8,4096]{1,0:T(8,128)(2,1)} %param.9), channel_id=1, source_target_pairs={{0,128},{1,129},{2,130},{3,131},{4,132},{5,133},{6,134},{7,135},{8... | collective-permute-start | bytes 196616 | tf_op jit(solution)/shard_map/ppermute | solution.py:25
  3.3 1.9 %collective-permute-start = (bf16[8,4096]{1,0:T(8,128)(2,1)}, bf16[8,4096]{1,0:T(8,128)(2,1)S(1)}, u32[]{:S(2)}, u32[]{:S(2)}) collective-permute-start(bf16[8,4096]{1,0:T(8,128)(2,1)} %param.9), channel_id=1, source_target_pairs={{0,64},{1,65},{2,66},{3,67},{4,68},{5,69},{6,70},{7,71},{8,72},{9,... | collective-permute-start | bytes 196616 | tf_op jit(solution)/shard_map/ppermute | solution.py:25
  5.2 0.0 collective-permute-start.2
  5.2 6.1 %shard_map.55 = bf16[512,128]{1,0:T(8,128)(2,1)} custom-call(s32[4]{0:T(128)} %lengths_ref.1, bf16[512,4096]{1,0:T(8,128)(2,1)} %inputs_ref.1, bf16[512,4096]{1,0:T(8,128)(2,1)} %cotangents_ref.1, bf16[4096,128]{1,0:T(8,128)(2,1)} %maps_ref.1), custom_call_target="tpu_custom_call" | custom-call | flops 1073741824 | bytes 8388608 | tf_op jit(solution)/shard_map/pallas_call | solution.py:70
  11.3 0.0 collective-permute-done
  11.3 0.2 collective-permute-done.2
  11.5 6.3 %collective-permute-start.6 = (bf16[512,128]{1,0:T(8,128)(2,1)}, bf16[512,128]{1,0:T(8,128)(2,1)S(1)}, u32[]{:S(2)}, u32[]{:S(2)}) collective-permute-start(bf16[512,128]{1,0:T(8,128)(2,1)} %shard_map.55), channel_id=1, source_target_pairs={{0,4},{1,5},{2,6},{3,7},{4,0},{5,1},{6,2},{7,3},{8,12},{9,13},{10,... | collective-permute-start | bytes 393224 | tf_op jit(solution)/shard_map/ppermute | solution.py:25
  17.8 0.9 %constant_dynamic-update-slice_fusion.1 = bf16[1024,128]{1,0:T(8,128)(2,1)S(1)} fusion(bf16[512,128]{1,0:T(8,128)(2,1)} %shard_map.55), kind=kLoop, calls=%fused_computation.3 | loop fusion | bytes 262144
  18.8 3.1 %collective-permute-done.6 = bf16[512,128]{1,0:T(8,128)(2,1)S(1)} collective-permute-done((bf16[512,128]{1,0:T(8,128)(2,1)}, bf16[512,128]{1,0:T(8,128)(2,1)S(1)}, u32[]{:S(2)}, u32[]{:S(2)}) %collective-permute-start.6) | collective-permute-done | bytes 131104 | tf_op jit(solution)/shard_map/ppermute | solution.py:25
  21.9 1.3 %collective-permute-start.9 = (bf16[1024,128]{1,0:T(8,128)(2,1)S(1)}, bf16[1024,128]{1,0:T(8,128)(2,1)S(1)}, u32[]{:S(2)}, u32[]{:S(2)}) collective-permute-start(bf16[1024,128]{1,0:T(8,128)(2,1)S(1)} %constant_dynamic-update-slice_fusion.refs_0_.rest_0_), channel_id=1, source_target_pairs={{0,3},{1,2},{2,1},{3,0},{4,7},{5,6},{6,5},{7,4},{8,11},{9,10},{10,... | collective-permute-start | bytes 786440 | tf_op jit(solution)/shard_map/ppermute | solution.py:25
  23.2 1.5 %collective-permute-start.8 = (bf16[1024,128]{1,0:T(8,128)(2,1)S(1)}, bf16[1024,128]{1,0:T(8,128)(2,1)S(1)}, u32[]{:S(2)}, u32[]{:S(2)}) collective-permute-start(bf16[1024,128]{1,0:T(8,128)(2,1)S(1)} %constant_dynamic-update-slice_fusion.refs_0_.rest_0_), channel_id=1, source_target_pairs={{0,2},{1,3},{2,0},{3,1},{4,6},{5,7},{6,4},{7,5},{8,10},{9,11},{10,... | collective-permute-start | bytes 786440 | tf_op jit(solution)/shard_map/ppermute | solution.py:25
  24.8 1.3 %collective-permute-start.7 = (bf16[1024,128]{1,0:T(8,128)(2,1)S(1)}, bf16[1024,128]{1,0:T(8,128)(2,1)S(1)}, u32[]{:S(2)}, u32[]{:S(2)}) collective-permute-start(bf16[1024,128]{1,0:T(8,128)(2,1)S(1)} %constant_dynamic-update-slice_fusion.refs_0_.rest_0_), channel_id=1, source_target_pairs={{0,1},{1,0},{2,3},{3,2},{4,5},{5,4},{6,7},{7,6},{8,9},{9,8},{10,11... | collective-permute-start | bytes 786440 | tf_op jit(solution)/shard_map/ppermute | solution.py:25
  26.1 2.8 %collective-permute-start.5 = (bf16[32,4096]{1,0:T(8,128)(2,1)S(1)}, bf16[32,4096]{1,0:T(8,128)(2,1)S(1)}, u32[]{:S(2)}, u32[]{:S(2)}) collective-permute-start(bf16[32,4096]{1,0:T(8,128)(2,1)S(1)} %pad_maximum_fusion), channel_id=1, source_target_pairs={{0,48},{1,49},{2,50},{3,51},{4,52},{5,53},{6,54},{7,55},{8,56},{9,... | collective-permute-start | bytes 786440 | tf_op jit(solution)/shard_map/ppermute | solution.py:25
  28.8 0.8 %collective-permute-start.4 = (bf16[32,4096]{1,0:T(8,128)(2,1)S(1)}, bf16[32,4096]{1,0:T(8,128)(2,1)S(1)}, u32[]{:S(2)}, u32[]{:S(2)}) collective-permute-start(bf16[32,4096]{1,0:T(8,128)(2,1)S(1)} %pad_maximum_fusion), channel_id=1, source_target_pairs={{0,32},{1,33},{2,34},{3,35},{4,36},{5,37},{6,38},{7,39},{8,40},{9,... | collective-permute-start | bytes 786440 | tf_op jit(solution)/shard_map/ppermute | solution.py:25
  29.6 4.7 %collective-permute-done.9.refs_3_.rest_3_ = bf16[1024,128]{1,0:T(8,128)(2,1)S(1)} collective-permute-done((bf16[1024,128]{1,0:T(8,128)(2,1)S(1)}, bf16[1024,128]{1,0:T(8,128)(2,1)S(1)}, u32[]{:S(2)}, u32[]{:S(2)}) %collective-permute-start.9) | collective-permute-done | bytes 262176 | tf_op jit(solution)/shard_map/ppermute | solution.py:25
  34.3 1.5 %collective-permute-start.3 = (bf16[32,4096]{1,0:T(8,128)(2,1)S(1)}, bf16[32,4096]{1,0:T(8,128)(2,1)S(1)}, u32[]{:S(2)}, u32[]{:S(2)}) collective-permute-start(bf16[32,4096]{1,0:T(8,128)(2,1)S(1)} %pad_maximum_fusion), channel_id=1, source_target_pairs={{0,16},{1,17},{2,18},{3,19},{4,20},{5,21},{6,22},{7,23},{8,24},{9,... | collective-permute-start | bytes 786440 | tf_op jit(solution)/shard_map/ppermute | solution.py:25
  35.8 0.0 collective-permute-done.8.refs_2_.rest_2_
  35.8 0.5 shard_map.56
  36.3 0.1 collective-permute-start.10
  36.4 1.2 %collective-permute-done.10 = f32[64,128]{1,0:T(8,128)S(1)} collective-permute-done((f32[64,128]{1,0:T(8,128)S(1)}, f32[64,128]{1,0:T(8,128)S(1)}, u32[]{:S(2)}, u32[]{:S(2)}) %collective-permute-start.10) | collective-permute-done | bytes 32800 | tf_op jit(solution)/shard_map/ppermute | solution.py:25
  37.6 0.1 collective-permute-start.11
  37.7 3.8 %collective-permute-done.11 = f32[64,128]{1,0:T(8,128)S(1)} collective-permute-done((f32[64,128]{1,0:T(8,128)S(1)}, f32[64,128]{1,0:T(8,128)S(1)}, u32[]{:S(2)}, u32[]{:S(2)}) %collective-permute-start.11) | collective-permute-done | bytes 32800 | tf_op jit(solution)/shard_map/ppermute | solution.py:25
  41.6 1.6 %collective-permute-start.12 = (f32[64,128]{1,0:T(8,128)S(1)}, f32[64,128]{1,0:T(8,128)S(1)}, u32[]{:S(2)}, u32[]{:S(2)}) collective-permute-start(f32[64,128]{1,0:T(8,128)S(1)} %add.19), channel_id=1, source_target_pairs={{0,128},{1,129},{2,130},{3,131},{4,132},{5,133},{6,134},{7,135},{8... | collective-permute-start | bytes 98312 | tf_op jit(solution)/shard_map/ppermute | solution.py:25
  43.2 3.5 %collective-permute-done.12 = f32[64,128]{1,0:T(8,128)S(1)} collective-permute-done((f32[64,128]{1,0:T(8,128)S(1)}, f32[64,128]{1,0:T(8,128)S(1)}, u32[]{:S(2)}, u32[]{:S(2)}) %collective-permute-start.12) | collective-permute-done | bytes 32800 | tf_op jit(solution)/shard_map/ppermute | solution.py:25
  46.9 0.1 collective-permute-start.16
  47.0 2.2 %collective-permute-start.15 = (f32[64,128]{1,0:T(8,128)S(1)}, f32[64,128]{1,0:T(8,128)S(1)}, u32[]{:S(2)}, u32[]{:S(2)}) collective-permute-start(f32[64,128]{1,0:T(8,128)S(1)} %add.20), channel_id=1, source_target_pairs={{0,48},{1,49},{2,50},{3,51},{4,52},{5,53},{6,54},{7,55},{8,56},{9,... | collective-permute-start | bytes 98312 | tf_op jit(solution)/shard_map/ppermute | solution.py:25
  49.1 0.9 %collective-permute-start.14 = (f32[64,128]{1,0:T(8,128)S(1)}, f32[64,128]{1,0:T(8,128)S(1)}, u32[]{:S(2)}, u32[]{:S(2)}) collective-permute-start(f32[64,128]{1,0:T(8,128)S(1)} %add.20), channel_id=1, source_target_pairs={{0,32},{1,33},{2,34},{3,35},{4,36},{5,37},{6,38},{7,39},{8,40},{9,... | collective-permute-start | bytes 98312 | tf_op jit(solution)/shard_map/ppermute | solution.py:25
  50.1 1.1 %collective-permute-start.13 = (f32[64,128]{1,0:T(8,128)S(1)}, f32[64,128]{1,0:T(8,128)S(1)}, u32[]{:S(2)}, u32[]{:S(2)}) collective-permute-start(f32[64,128]{1,0:T(8,128)S(1)} %add.20), channel_id=1, source_target_pairs={{0,16},{1,17},{2,18},{3,19},{4,20},{5,21},{6,22},{7,23},{8,24},{9,... | collective-permute-start | bytes 98312 | tf_op jit(solution)/shard_map/ppermute | solution.py:25
  51.1 0.1 pad_add_fusion.place_ref
  51.2 1.0 %collective-permute-done.15 = f32[64,128]{1,0:T(8,128)S(1)} collective-permute-done((f32[64,128]{1,0:T(8,128)S(1)}, f32[64,128]{1,0:T(8,128)S(1)}, u32[]{:S(2)}, u32[]{:S(2)}) %collective-permute-start.15) | collective-permute-done | bytes 32800 | tf_op jit(solution)/shard_map/ppermute | solution.py:25
  52.2 2.6 %collective-permute-done.14 = f32[64,128]{1,0:T(8,128)S(1)} collective-permute-done((f32[64,128]{1,0:T(8,128)S(1)}, f32[64,128]{1,0:T(8,128)S(1)}, u32[]{:S(2)}, u32[]{:S(2)}) %collective-permute-start.14) | collective-permute-done | bytes 32800 | tf_op jit(solution)/shard_map/ppermute | solution.py:25
  54.8 15.0 %shard_map.57 = f32[4096,256]{1,0:T(8,128)} custom-call(s32[2]{0:T(128)S(1)} %pad_add_fusion.place_ref, f32[64,128]{1,0:T(8,128)S(1)} %add_add_fusion.sums_ref, bf16[128,4096]{1,0:T(8,128)(2,1)S(1)} %constant_dynamic-update-slice_fusion.2.near_ref, bf16[128,4096]{1,0:T(8,128)(2,1)S(1)} %collective-permute-done.16.far_ref, ...), custom_call_target="tpu_custom_call" | custom-call | flops 8589934592 | bytes 4194304 | tf_op jit(solution)/shard_map/pallas_call | solution.py:233
  (19 shorter events, 0.2 us)
Async XLA Ops:
  0.0 11.5 %copy-start = (bf16[8,4096]{1,0:T(8,128)(2,1)S(1)}, bf16[8,4096]{1,0:T(8,128)(2,1)}, u32[]{:S(2)}) copy-start(bf16[8,4096]{1,0:T(8,128)(2,1)} %param.9) | copy-start | bytes 196612
  0.0 11.3 %collective-permute-start.1 = (bf16[8,4096]{1,0:T(8,128)(2,1)}, bf16[8,4096]{1,0:T(8,128)(2,1)S(1)}, u32[]{:S(2)}, u32[]{:S(2)}) collective-permute-start(bf16[8,4096]{1,0:T(8,128)(2,1)} %param.9), channel_id=1, source_target_pairs={{0,128},{1,129},{2,130},{3,131},{4,132},{5,133},{6,134},{7,135},{8... | collective-permute-start | bytes 196616 | tf_op jit(solution)/shard_map/ppermute | solution.py:25
  3.3 8.0 %collective-permute-start = (bf16[8,4096]{1,0:T(8,128)(2,1)}, bf16[8,4096]{1,0:T(8,128)(2,1)S(1)}, u32[]{:S(2)}, u32[]{:S(2)}) collective-permute-start(bf16[8,4096]{1,0:T(8,128)(2,1)} %param.9), channel_id=1, source_target_pairs={{0,64},{1,65},{2,66},{3,67},{4,68},{5,69},{6,70},{7,71},{8,72},{9,... | collective-permute-start | bytes 196616 | tf_op jit(solution)/shard_map/ppermute | solution.py:25
  5.2 6.3 %collective-permute-start.2 = (bf16[8,4096]{1,0:T(8,128)(2,1)}, bf16[8,4096]{1,0:T(8,128)(2,1)S(1)}, u32[]{:S(2)}, u32[]{:S(2)}) collective-permute-start(bf16[8,4096]{1,0:T(8,128)(2,1)} %param.9), channel_id=1, source_target_pairs={{0,192},{1,193},{2,194},{3,195},{4,196},{5,197},{6,198},{7,199},{8... | collective-permute-start | bytes 196616 | tf_op jit(solution)/shard_map/ppermute | solution.py:25
  11.5 10.4 %collective-permute-start.6 = (bf16[512,128]{1,0:T(8,128)(2,1)}, bf16[512,128]{1,0:T(8,128)(2,1)S(1)}, u32[]{:S(2)}, u32[]{:S(2)}) collective-permute-start(bf16[512,128]{1,0:T(8,128)(2,1)} %shard_map.55), channel_id=1, source_target_pairs={{0,4},{1,5},{2,6},{3,7},{4,0},{5,1},{6,2},{7,3},{8,12},{9,13},{10,... | collective-permute-start | bytes 393224 | tf_op jit(solution)/shard_map/ppermute | solution.py:25
  21.9 12.5 %collective-permute-start.9 = (bf16[1024,128]{1,0:T(8,128)(2,1)S(1)}, bf16[1024,128]{1,0:T(8,128)(2,1)S(1)}, u32[]{:S(2)}, u32[]{:S(2)}) collective-permute-start(bf16[1024,128]{1,0:T(8,128)(2,1)S(1)} %constant_dynamic-update-slice_fusion.refs_0_.rest_0_), channel_id=1, source_target_pairs={{0,3},{1,2},{2,1},{3,0},{4,7},{5,6},{6,5},{7,4},{8,11},{9,10},{10,... | collective-permute-start | bytes 786440 | tf_op jit(solution)/shard_map/ppermute | solution.py:25
  23.2 12.6 %collective-permute-start.8 = (bf16[1024,128]{1,0:T(8,128)(2,1)S(1)}, bf16[1024,128]{1,0:T(8,128)(2,1)S(1)}, u32[]{:S(2)}, u32[]{:S(2)}) collective-permute-start(bf16[1024,128]{1,0:T(8,128)(2,1)S(1)} %constant_dynamic-update-slice_fusion.refs_0_.rest_0_), channel_id=1, source_target_pairs={{0,2},{1,3},{2,0},{3,1},{4,6},{5,7},{6,4},{7,5},{8,10},{9,11},{10,... | collective-permute-start | bytes 786440 | tf_op jit(solution)/shard_map/ppermute | solution.py:25
  24.8 11.1 %collective-permute-start.7 = (bf16[1024,128]{1,0:T(8,128)(2,1)S(1)}, bf16[1024,128]{1,0:T(8,128)(2,1)S(1)}, u32[]{:S(2)}, u32[]{:S(2)}) collective-permute-start(bf16[1024,128]{1,0:T(8,128)(2,1)S(1)} %constant_dynamic-update-slice_fusion.refs_0_.rest_0_), channel_id=1, source_target_pairs={{0,1},{1,0},{2,3},{3,2},{4,5},{5,4},{6,7},{7,6},{8,9},{9,8},{10,11... | collective-permute-start | bytes 786440 | tf_op jit(solution)/shard_map/ppermute | solution.py:25
  26.1 20.7 %collective-permute-start.5 = (bf16[32,4096]{1,0:T(8,128)(2,1)S(1)}, bf16[32,4096]{1,0:T(8,128)(2,1)S(1)}, u32[]{:S(2)}, u32[]{:S(2)}) collective-permute-start(bf16[32,4096]{1,0:T(8,128)(2,1)S(1)} %pad_maximum_fusion), channel_id=1, source_target_pairs={{0,48},{1,49},{2,50},{3,51},{4,52},{5,53},{6,54},{7,55},{8,56},{9,... | collective-permute-start | bytes 786440 | tf_op jit(solution)/shard_map/ppermute | solution.py:25
  28.8 17.9 %collective-permute-start.4 = (bf16[32,4096]{1,0:T(8,128)(2,1)S(1)}, bf16[32,4096]{1,0:T(8,128)(2,1)S(1)}, u32[]{:S(2)}, u32[]{:S(2)}) collective-permute-start(bf16[32,4096]{1,0:T(8,128)(2,1)S(1)} %pad_maximum_fusion), channel_id=1, source_target_pairs={{0,32},{1,33},{2,34},{3,35},{4,36},{5,37},{6,38},{7,39},{8,40},{9,... | collective-permute-start | bytes 786440 | tf_op jit(solution)/shard_map/ppermute | solution.py:25
  34.3 12.4 %collective-permute-start.3 = (bf16[32,4096]{1,0:T(8,128)(2,1)S(1)}, bf16[32,4096]{1,0:T(8,128)(2,1)S(1)}, u32[]{:S(2)}, u32[]{:S(2)}) collective-permute-start(bf16[32,4096]{1,0:T(8,128)(2,1)S(1)} %pad_maximum_fusion), channel_id=1, source_target_pairs={{0,16},{1,17},{2,18},{3,19},{4,20},{5,21},{6,22},{7,23},{8,24},{9,... | collective-permute-start | bytes 786440 | tf_op jit(solution)/shard_map/ppermute | solution.py:25
  36.3 1.3 %collective-permute-start.10 = (f32[64,128]{1,0:T(8,128)S(1)}, f32[64,128]{1,0:T(8,128)S(1)}, u32[]{:S(2)}, u32[]{:S(2)}) collective-permute-start(f32[64,128]{1,0:T(8,128)S(1)} %shard_map.56), channel_id=1, source_target_pairs={{0,8},{1,9},{2,10},{3,11},{4,12},{5,13},{6,14},{7,15},{8,0},{9,1},... | collective-permute-start | bytes 98312 | tf_op jit(solution)/shard_map/ppermute | solution.py:25
  37.6 3.9 %collective-permute-start.11 = (f32[64,128]{1,0:T(8,128)S(1)}, f32[64,128]{1,0:T(8,128)S(1)}, u32[]{:S(2)}, u32[]{:S(2)}) collective-permute-start(f32[64,128]{1,0:T(8,128)S(1)} %add.18), channel_id=1, source_target_pairs={{0,64},{1,65},{2,66},{3,67},{4,68},{5,69},{6,70},{7,71},{8,72},{9,... | collective-permute-start | bytes 98312 | tf_op jit(solution)/shard_map/ppermute | solution.py:25
  41.6 5.2 %collective-permute-start.12 = (f32[64,128]{1,0:T(8,128)S(1)}, f32[64,128]{1,0:T(8,128)S(1)}, u32[]{:S(2)}, u32[]{:S(2)}) collective-permute-start(f32[64,128]{1,0:T(8,128)S(1)} %add.19), channel_id=1, source_target_pairs={{0,128},{1,129},{2,130},{3,131},{4,132},{5,133},{6,134},{7,135},{8... | collective-permute-start | bytes 98312 | tf_op jit(solution)/shard_map/ppermute | solution.py:25
  46.9 8.0 %collective-permute-start.16 = (bf16[128,4096]{1,0:T(8,128)(2,1)S(1)}, bf16[128,4096]{1,0:T(8,128)(2,1)S(1)}, u32[]{:S(2)}, u32[]{:S(2)}) collective-permute-start(bf16[128,4096]{1,0:T(8,128)(2,1)S(1)} %constant_dynamic-update-slice_fusion.2.near_ref), channel_id=1, source_target_pairs={{0,8},{1,9},{2,10},{3,11},{4,12},{5,13},{6,14},{7,15},{8,0},{9,1},... | collective-permute-start | bytes 3145736 | tf_op jit(solution)/shard_map/ppermute | solution.py:25
  47.0 5.2 %collective-permute-start.15 = (f32[64,128]{1,0:T(8,128)S(1)}, f32[64,128]{1,0:T(8,128)S(1)}, u32[]{:S(2)}, u32[]{:S(2)}) collective-permute-start(f32[64,128]{1,0:T(8,128)S(1)} %add.20), channel_id=1, source_target_pairs={{0,48},{1,49},{2,50},{3,51},{4,52},{5,53},{6,54},{7,55},{8,56},{9,... | collective-permute-start | bytes 98312 | tf_op jit(solution)/shard_map/ppermute | solution.py:25
  49.1 5.7 %collective-permute-start.14 = (f32[64,128]{1,0:T(8,128)S(1)}, f32[64,128]{1,0:T(8,128)S(1)}, u32[]{:S(2)}, u32[]{:S(2)}) collective-permute-start(f32[64,128]{1,0:T(8,128)S(1)} %add.20), channel_id=1, source_target_pairs={{0,32},{1,33},{2,34},{3,35},{4,36},{5,37},{6,38},{7,39},{8,40},{9,... | collective-permute-start | bytes 98312 | tf_op jit(solution)/shard_map/ppermute | solution.py:25
  50.1 4.8 %collective-permute-start.13 = (f32[64,128]{1,0:T(8,128)S(1)}, f32[64,128]{1,0:T(8,128)S(1)}, u32[]{:S(2)}, u32[]{:S(2)}) collective-permute-start(f32[64,128]{1,0:T(8,128)S(1)} %add.20), channel_id=1, source_target_pairs={{0,16},{1,17},{2,18},{3,19},{4,20},{5,21},{6,22},{7,23},{8,24},{9,... | collective-permute-start | bytes 98312 | tf_op jit(solution)/shard_map/ppermute | solution.py:25

commit v5 on v4

--- a/solution.py
+++ b/solution.py
@@ -225,7 +225,7 @@
             written(round_, h).wait()
 
 
-def scores_of(place, sums, near, far, parts, tile=256, together=4):
+def scores_of(place, sums, near, far, parts, tile=256, together=8):
     both = sums.shape[1]
     number, entries = 2 * near.shape[0], near.shape[1]
     rows = sum(part.shape[0] for part in parts)

time: 70.2 us -> 69.5 us (0.990)
  transfers between devices with their start and end apart: 17 -> 17, of which waited for: 8 -> 8; matrix products, arithmetic and copies ran while one was open for 1% -> 2% of each run, Pallas kernels for 9% -> 9%
where the time goes in v5:
time: 69.5 us; the launch traced here: 69.4 us
  starting transfers between devices  26.8 us (39%)
  Pallas kernels  20.9 us (30%)
  waiting for transfers between devices  20.2 us (29%)
  local copies, waits for them, and re-layouts  1.05 us (2%)
    ppermute x17, starting transfers between devices, exchange(): return lax.ppermute(array, BOTH, pairs)  26.8 us
    ppermute x17, waiting for transfers between devices, exchange(): return lax.ppermute(array, BOTH, pairs)  20.2 us
    pallas_call x1, Pallas kernels, scores_of(): pl.pallas_call(functools.partial(scores_kernel, tile=tile, together=toget...  14.3 us
    pallas_call x1, Pallas kernels, sides_of(): pl.pallas_call(sides_kernel, in_specs=[pl.BlockSpec(memory_space=pltpu.SM...  6.06 us
  transfers between devices with their start and end apart: 17, of which 8 were waited for; matrix products, arithmetic and copies ran while one was open for 2% of the time, Pallas kernels for 9%

profile of v5, /device:TPU:24, one launch (start us, length us, event | category | flops | bytes accessed | tf_op | source)
XLA Modules:
  0.0 69.4 jit_solution(16607293746269313323)
XLA Ops:
  0.0 3.3 %collective-permute-start.1 = (bf16[8,4096]{1,0:T(8,128)(2,1)}, bf16[8,4096]{1,0:T(8,128)(2,1)S(1)}, u32[]{:S(2)}, u32[]{:S(2)}) collective-permute-start(bf16[8,4096]{1,0:T(8,128)(2,1)} %param.9), channel_id=1, source_target_pairs={{0,128},{1,129},{2,130},{3,131},{4,132},{5,133},{6,134},{7,135},{8... | collective-permute-start | bytes 196616 | tf_op jit(solution)/shard_map/ppermute | solution.py:25
  3.3 1.9 %collective-permute-start = (bf16[8,4096]{1,0:T(8,128)(2,1)}, bf16[8,4096]{1,0:T(8,128)(2,1)S(1)}, u32[]{:S(2)}, u32[]{:S(2)}) collective-permute-start(bf16[8,4096]{1,0:T(8,128)(2,1)} %param.9), channel_id=1, source_target_pairs={{0,64},{1,65},{2,66},{3,67},{4,68},{5,69},{6,70},{7,71},{8,72},{9,... | collective-permute-start | bytes 196616 | tf_op jit(solution)/shard_map/ppermute | solution.py:25
  5.2 0.0 collective-permute-start.2
  5.2 6.1 %shard_map.55 = bf16[512,128]{1,0:T(8,128)(2,1)} custom-call(s32[4]{0:T(128)} %lengths_ref.1, bf16[512,4096]{1,0:T(8,128)(2,1)} %inputs_ref.1, bf16[512,4096]{1,0:T(8,128)(2,1)} %cotangents_ref.1, bf16[4096,128]{1,0:T(8,128)(2,1)} %maps_ref.1), custom_call_target="tpu_custom_call" | custom-call | flops 1073741824 | bytes 8388608 | tf_op jit(solution)/shard_map/pallas_call | solution.py:70
  11.3 0.2 collective-permute-done.2
  11.5 6.3 %collective-permute-start.6 = (bf16[512,128]{1,0:T(8,128)(2,1)}, bf16[512,128]{1,0:T(8,128)(2,1)S(1)}, u32[]{:S(2)}, u32[]{:S(2)}) collective-permute-start(bf16[512,128]{1,0:T(8,128)(2,1)} %shard_map.55), channel_id=1, source_target_pairs={{0,4},{1,5},{2,6},{3,7},{4,0},{5,1},{6,2},{7,3},{8,12},{9,13},{10,... | collective-permute-start | bytes 393224 | tf_op jit(solution)/shard_map/ppermute | solution.py:25
  17.8 0.9 %constant_dynamic-update-slice_fusion.1 = bf16[1024,128]{1,0:T(8,128)(2,1)S(1)} fusion(bf16[512,128]{1,0:T(8,128)(2,1)} %shard_map.55), kind=kLoop, calls=%fused_computation.3 | loop fusion | bytes 262144
  18.8 3.1 %collective-permute-done.6 = bf16[512,128]{1,0:T(8,128)(2,1)S(1)} collective-permute-done((bf16[512,128]{1,0:T(8,128)(2,1)}, bf16[512,128]{1,0:T(8,128)(2,1)S(1)}, u32[]{:S(2)}, u32[]{:S(2)}) %collective-permute-start.6) | collective-permute-done | bytes 131104 | tf_op jit(solution)/shard_map/ppermute | solution.py:25
  21.9 1.3 %collective-permute-start.9 = (bf16[1024,128]{1,0:T(8,128)(2,1)S(1)}, bf16[1024,128]{1,0:T(8,128)(2,1)S(1)}, u32[]{:S(2)}, u32[]{:S(2)}) collective-permute-start(bf16[1024,128]{1,0:T(8,128)(2,1)S(1)} %constant_dynamic-update-slice_fusion.refs_0_.rest_0_), channel_id=1, source_target_pairs={{0,3},{1,2},{2,1},{3,0},{4,7},{5,6},{6,5},{7,4},{8,11},{9,10},{10,... | collective-permute-start | bytes 786440 | tf_op jit(solution)/shard_map/ppermute | solution.py:25
  23.2 1.5 %collective-permute-start.8 = (bf16[1024,128]{1,0:T(8,128)(2,1)S(1)}, bf16[1024,128]{1,0:T(8,128)(2,1)S(1)}, u32[]{:S(2)}, u32[]{:S(2)}) collective-permute-start(bf16[1024,128]{1,0:T(8,128)(2,1)S(1)} %constant_dynamic-update-slice_fusion.refs_0_.rest_0_), channel_id=1, source_target_pairs={{0,2},{1,3},{2,0},{3,1},{4,6},{5,7},{6,4},{7,5},{8,10},{9,11},{10,... | collective-permute-start | bytes 786440 | tf_op jit(solution)/shard_map/ppermute | solution.py:25
  24.8 1.3 %collective-permute-start.7 = (bf16[1024,128]{1,0:T(8,128)(2,1)S(1)}, bf16[1024,128]{1,0:T(8,128)(2,1)S(1)}, u32[]{:S(2)}, u32[]{:S(2)}) collective-permute-start(bf16[1024,128]{1,0:T(8,128)(2,1)S(1)} %constant_dynamic-update-slice_fusion.refs_0_.rest_0_), channel_id=1, source_target_pairs={{0,1},{1,0},{2,3},{3,2},{4,5},{5,4},{6,7},{7,6},{8,9},{9,8},{10,11... | collective-permute-start | bytes 786440 | tf_op jit(solution)/shard_map/ppermute | solution.py:25
  26.1 2.8 %collective-permute-start.5 = (bf16[32,4096]{1,0:T(8,128)(2,1)S(1)}, bf16[32,4096]{1,0:T(8,128)(2,1)S(1)}, u32[]{:S(2)}, u32[]{:S(2)}) collective-permute-start(bf16[32,4096]{1,0:T(8,128)(2,1)S(1)} %pad_maximum_fusion), channel_id=1, source_target_pairs={{0,48},{1,49},{2,50},{3,51},{4,52},{5,53},{6,54},{7,55},{8,56},{9,... | collective-permute-start | bytes 786440 | tf_op jit(solution)/shard_map/ppermute | solution.py:25
  28.8 0.8 %collective-permute-start.4 = (bf16[32,4096]{1,0:T(8,128)(2,1)S(1)}, bf16[32,4096]{1,0:T(8,128)(2,1)S(1)}, u32[]{:S(2)}, u32[]{:S(2)}) collective-permute-start(bf16[32,4096]{1,0:T(8,128)(2,1)S(1)} %pad_maximum_fusion), channel_id=1, source_target_pairs={{0,32},{1,33},{2,34},{3,35},{4,36},{5,37},{6,38},{7,39},{8,40},{9,... | collective-permute-start | bytes 786440 | tf_op jit(solution)/shard_map/ppermute | solution.py:25
  29.6 4.7 %collective-permute-done.9.refs_3_.rest_3_ = bf16[1024,128]{1,0:T(8,128)(2,1)S(1)} collective-permute-done((bf16[1024,128]{1,0:T(8,128)(2,1)S(1)}, bf16[1024,128]{1,0:T(8,128)(2,1)S(1)}, u32[]{:S(2)}, u32[]{:S(2)}) %collective-permute-start.9) | collective-permute-done | bytes 262176 | tf_op jit(solution)/shard_map/ppermute | solution.py:25
  34.3 1.5 %collective-permute-start.3 = (bf16[32,4096]{1,0:T(8,128)(2,1)S(1)}, bf16[32,4096]{1,0:T(8,128)(2,1)S(1)}, u32[]{:S(2)}, u32[]{:S(2)}) collective-permute-start(bf16[32,4096]{1,0:T(8,128)(2,1)S(1)} %pad_maximum_fusion), channel_id=1, source_target_pairs={{0,16},{1,17},{2,18},{3,19},{4,20},{5,21},{6,22},{7,23},{8,24},{9,... | collective-permute-start | bytes 786440 | tf_op jit(solution)/shard_map/ppermute | solution.py:25
  35.8 0.0 collective-permute-done.8.refs_2_.rest_2_
  35.8 0.5 shard_map.56
  36.3 0.1 collective-permute-start.10
  36.4 1.2 %collective-permute-done.10 = f32[64,128]{1,0:T(8,128)S(1)} collective-permute-done((f32[64,128]{1,0:T(8,128)S(1)}, f32[64,128]{1,0:T(8,128)S(1)}, u32[]{:S(2)}, u32[]{:S(2)}) %collective-permute-start.10) | collective-permute-done | bytes 32800 | tf_op jit(solution)/shard_map/ppermute | solution.py:25
  37.6 0.1 collective-permute-start.11
  37.7 3.8 %collective-permute-done.11 = f32[64,128]{1,0:T(8,128)S(1)} collective-permute-done((f32[64,128]{1,0:T(8,128)S(1)}, f32[64,128]{1,0:T(8,128)S(1)}, u32[]{:S(2)}, u32[]{:S(2)}) %collective-permute-start.11) | collective-permute-done | bytes 32800 | tf_op jit(solution)/shard_map/ppermute | solution.py:25
  41.6 1.6 %collective-permute-start.12 = (f32[64,128]{1,0:T(8,128)S(1)}, f32[64,128]{1,0:T(8,128)S(1)}, u32[]{:S(2)}, u32[]{:S(2)}) collective-permute-start(f32[64,128]{1,0:T(8,128)S(1)} %add.19), channel_id=1, source_target_pairs={{0,128},{1,129},{2,130},{3,131},{4,132},{5,133},{6,134},{7,135},{8... | collective-permute-start | bytes 98312 | tf_op jit(solution)/shard_map/ppermute | solution.py:25
  43.2 3.5 %collective-permute-done.12 = f32[64,128]{1,0:T(8,128)S(1)} collective-permute-done((f32[64,128]{1,0:T(8,128)S(1)}, f32[64,128]{1,0:T(8,128)S(1)}, u32[]{:S(2)}, u32[]{:S(2)}) %collective-permute-start.12) | collective-permute-done | bytes 32800 | tf_op jit(solution)/shard_map/ppermute | solution.py:25
  46.7 0.0 collective-permute-done.5
  46.9 0.1 collective-permute-start.16
  47.0 2.2 %collective-permute-start.15 = (f32[64,128]{1,0:T(8,128)S(1)}, f32[64,128]{1,0:T(8,128)S(1)}, u32[]{:S(2)}, u32[]{:S(2)}) collective-permute-start(f32[64,128]{1,0:T(8,128)S(1)} %add.20), channel_id=1, source_target_pairs={{0,48},{1,49},{2,50},{3,51},{4,52},{5,53},{6,54},{7,55},{8,56},{9,... | collective-permute-start | bytes 98312 | tf_op jit(solution)/shard_map/ppermute | solution.py:25
  49.1 0.9 %collective-permute-start.14 = (f32[64,128]{1,0:T(8,128)S(1)}, f32[64,128]{1,0:T(8,128)S(1)}, u32[]{:S(2)}, u32[]{:S(2)}) collective-permute-start(f32[64,128]{1,0:T(8,128)S(1)} %add.20), channel_id=1, source_target_pairs={{0,32},{1,33},{2,34},{3,35},{4,36},{5,37},{6,38},{7,39},{8,40},{9,... | collective-permute-start | bytes 98312 | tf_op jit(solution)/shard_map/ppermute | solution.py:25
  50.1 1.1 %collective-permute-start.13 = (f32[64,128]{1,0:T(8,128)S(1)}, f32[64,128]{1,0:T(8,128)S(1)}, u32[]{:S(2)}, u32[]{:S(2)}) collective-permute-start(f32[64,128]{1,0:T(8,128)S(1)} %add.20), channel_id=1, source_target_pairs={{0,16},{1,17},{2,18},{3,19},{4,20},{5,21},{6,22},{7,23},{8,24},{9,... | collective-permute-start | bytes 98312 | tf_op jit(solution)/shard_map/ppermute | solution.py:25
  51.1 0.1 pad_add_fusion.place_ref
  51.2 1.0 %collective-permute-done.15 = f32[64,128]{1,0:T(8,128)S(1)} collective-permute-done((f32[64,128]{1,0:T(8,128)S(1)}, f32[64,128]{1,0:T(8,128)S(1)}, u32[]{:S(2)}, u32[]{:S(2)}) %collective-permute-start.15) | collective-permute-done | bytes 32800 | tf_op jit(solution)/shard_map/ppermute | solution.py:25
  52.2 2.6 %collective-permute-done.14 = f32[64,128]{1,0:T(8,128)S(1)} collective-permute-done((f32[64,128]{1,0:T(8,128)S(1)}, f32[64,128]{1,0:T(8,128)S(1)}, u32[]{:S(2)}, u32[]{:S(2)}) %collective-permute-start.14) | collective-permute-done | bytes 32800 | tf_op jit(solution)/shard_map/ppermute | solution.py:25
  54.8 14.3 %shard_map.57 = f32[4096,256]{1,0:T(8,128)} custom-call(s32[2]{0:T(128)S(1)} %pad_add_fusion.place_ref, f32[64,128]{1,0:T(8,128)S(1)} %add_add_fusion.sums_ref, bf16[128,4096]{1,0:T(8,128)(2,1)S(1)} %constant_dynamic-update-slice_fusion.2.near_ref, bf16[128,4096]{1,0:T(8,128)(2,1)S(1)} %collective-permute-done.16.far_ref, ...), custom_call_target="tpu_custom_call" | custom-call | flops 8589934592 | bytes 4194304 | tf_op jit(solution)/shard_map/pallas_call | solution.py:233
  (19 shorter events, 0.2 us)
Async XLA Ops:
  0.0 11.5 %copy-start = (bf16[8,4096]{1,0:T(8,128)(2,1)S(1)}, bf16[8,4096]{1,0:T(8,128)(2,1)}, u32[]{:S(2)}) copy-start(bf16[8,4096]{1,0:T(8,128)(2,1)} %param.9) | copy-start | bytes 196612
  0.0 11.3 %collective-permute-start.1 = (bf16[8,4096]{1,0:T(8,128)(2,1)}, bf16[8,4096]{1,0:T(8,128)(2,1)S(1)}, u32[]{:S(2)}, u32[]{:S(2)}) collective-permute-start(bf16[8,4096]{1,0:T(8,128)(2,1)} %param.9), channel_id=1, source_target_pairs={{0,128},{1,129},{2,130},{3,131},{4,132},{5,133},{6,134},{7,135},{8... | collective-permute-start | bytes 196616 | tf_op jit(solution)/shard_map/ppermute | solution.py:25
  3.3 8.0 %collective-permute-start = (bf16[8,4096]{1,0:T(8,128)(2,1)}, bf16[8,4096]{1,0:T(8,128)(2,1)S(1)}, u32[]{:S(2)}, u32[]{:S(2)}) collective-permute-start(bf16[8,4096]{1,0:T(8,128)(2,1)} %param.9), channel_id=1, source_target_pairs={{0,64},{1,65},{2,66},{3,67},{4,68},{5,69},{6,70},{7,71},{8,72},{9,... | collective-permute-start | bytes 196616 | tf_op jit(solution)/shard_map/ppermute | solution.py:25
  5.2 6.3 %collective-permute-start.2 = (bf16[8,4096]{1,0:T(8,128)(2,1)}, bf16[8,4096]{1,0:T(8,128)(2,1)S(1)}, u32[]{:S(2)}, u32[]{:S(2)}) collective-permute-start(bf16[8,4096]{1,0:T(8,128)(2,1)} %param.9), channel_id=1, source_target_pairs={{0,192},{1,193},{2,194},{3,195},{4,196},{5,197},{6,198},{7,199},{8... | collective-permute-start | bytes 196616 | tf_op jit(solution)/shard_map/ppermute | solution.py:25
  11.5 10.4 %collective-permute-start.6 = (bf16[512,128]{1,0:T(8,128)(2,1)}, bf16[512,128]{1,0:T(8,128)(2,1)S(1)}, u32[]{:S(2)}, u32[]{:S(2)}) collective-permute-start(bf16[512,128]{1,0:T(8,128)(2,1)} %shard_map.55), channel_id=1, source_target_pairs={{0,4},{1,5},{2,6},{3,7},{4,0},{5,1},{6,2},{7,3},{8,12},{9,13},{10,... | collective-permute-start | bytes 393224 | tf_op jit(solution)/shard_map/ppermute | solution.py:25
  21.9 12.5 %collective-permute-start.9 = (bf16[1024,128]{1,0:T(8,128)(2,1)S(1)}, bf16[1024,128]{1,0:T(8,128)(2,1)S(1)}, u32[]{:S(2)}, u32[]{:S(2)}) collective-permute-start(bf16[1024,128]{1,0:T(8,128)(2,1)S(1)} %constant_dynamic-update-slice_fusion.refs_0_.rest_0_), channel_id=1, source_target_pairs={{0,3},{1,2},{2,1},{3,0},{4,7},{5,6},{6,5},{7,4},{8,11},{9,10},{10,... | collective-permute-start | bytes 786440 | tf_op jit(solution)/shard_map/ppermute | solution.py:25
  23.2 12.6 %collective-permute-start.8 = (bf16[1024,128]{1,0:T(8,128)(2,1)S(1)}, bf16[1024,128]{1,0:T(8,128)(2,1)S(1)}, u32[]{:S(2)}, u32[]{:S(2)}) collective-permute-start(bf16[1024,128]{1,0:T(8,128)(2,1)S(1)} %constant_dynamic-update-slice_fusion.refs_0_.rest_0_), channel_id=1, source_target_pairs={{0,2},{1,3},{2,0},{3,1},{4,6},{5,7},{6,4},{7,5},{8,10},{9,11},{10,... | collective-permute-start | bytes 786440 | tf_op jit(solution)/shard_map/ppermute | solution.py:25
  24.8 11.1 %collective-permute-start.7 = (bf16[1024,128]{1,0:T(8,128)(2,1)S(1)}, bf16[1024,128]{1,0:T(8,128)(2,1)S(1)}, u32[]{:S(2)}, u32[]{:S(2)}) collective-permute-start(bf16[1024,128]{1,0:T(8,128)(2,1)S(1)} %constant_dynamic-update-slice_fusion.refs_0_.rest_0_), channel_id=1, source_target_pairs={{0,1},{1,0},{2,3},{3,2},{4,5},{5,4},{6,7},{7,6},{8,9},{9,8},{10,11... | collective-permute-start | bytes 786440 | tf_op jit(solution)/shard_map/ppermute | solution.py:25
  26.1 20.7 %collective-permute-start.5 = (bf16[32,4096]{1,0:T(8,128)(2,1)S(1)}, bf16[32,4096]{1,0:T(8,128)(2,1)S(1)}, u32[]{:S(2)}, u32[]{:S(2)}) collective-permute-start(bf16[32,4096]{1,0:T(8,128)(2,1)S(1)} %pad_maximum_fusion), channel_id=1, source_target_pairs={{0,48},{1,49},{2,50},{3,51},{4,52},{5,53},{6,54},{7,55},{8,56},{9,... | collective-permute-start | bytes 786440 | tf_op jit(solution)/shard_map/ppermute | solution.py:25
  28.8 17.9 %collective-permute-start.4 = (bf16[32,4096]{1,0:T(8,128)(2,1)S(1)}, bf16[32,4096]{1,0:T(8,128)(2,1)S(1)}, u32[]{:S(2)}, u32[]{:S(2)}) collective-permute-start(bf16[32,4096]{1,0:T(8,128)(2,1)S(1)} %pad_maximum_fusion), channel_id=1, source_target_pairs={{0,32},{1,33},{2,34},{3,35},{4,36},{5,37},{6,38},{7,39},{8,40},{9,... | collective-permute-start | bytes 786440 | tf_op jit(solution)/shard_map/ppermute | solution.py:25
  34.3 12.4 %collective-permute-start.3 = (bf16[32,4096]{1,0:T(8,128)(2,1)S(1)}, bf16[32,4096]{1,0:T(8,128)(2,1)S(1)}, u32[]{:S(2)}, u32[]{:S(2)}) collective-permute-start(bf16[32,4096]{1,0:T(8,128)(2,1)S(1)} %pad_maximum_fusion), channel_id=1, source_target_pairs={{0,16},{1,17},{2,18},{3,19},{4,20},{5,21},{6,22},{7,23},{8,24},{9,... | collective-permute-start | bytes 786440 | tf_op jit(solution)/shard_map/ppermute | solution.py:25
  36.3 1.3 %collective-permute-start.10 = (f32[64,128]{1,0:T(8,128)S(1)}, f32[64,128]{1,0:T(8,128)S(1)}, u32[]{:S(2)}, u32[]{:S(2)}) collective-permute-start(f32[64,128]{1,0:T(8,128)S(1)} %shard_map.56), channel_id=1, source_target_pairs={{0,8},{1,9},{2,10},{3,11},{4,12},{5,13},{6,14},{7,15},{8,0},{9,1},... | collective-permute-start | bytes 98312 | tf_op jit(solution)/shard_map/ppermute | solution.py:25
  37.6 3.9 %collective-permute-start.11 = (f32[64,128]{1,0:T(8,128)S(1)}, f32[64,128]{1,0:T(8,128)S(1)}, u32[]{:S(2)}, u32[]{:S(2)}) collective-permute-start(f32[64,128]{1,0:T(8,128)S(1)} %add.18), channel_id=1, source_target_pairs={{0,64},{1,65},{2,66},{3,67},{4,68},{5,69},{6,70},{7,71},{8,72},{9,... | collective-permute-start | bytes 98312 | tf_op jit(solution)/shard_map/ppermute | solution.py:25
  41.6 5.2 %collective-permute-start.12 = (f32[64,128]{1,0:T(8,128)S(1)}, f32[64,128]{1,0:T(8,128)S(1)}, u32[]{:S(2)}, u32[]{:S(2)}) collective-permute-start(f32[64,128]{1,0:T(8,128)S(1)} %add.19), channel_id=1, source_target_pairs={{0,128},{1,129},{2,130},{3,131},{4,132},{5,133},{6,134},{7,135},{8... | collective-permute-start | bytes 98312 | tf_op jit(solution)/shard_map/ppermute | solution.py:25
  46.9 8.0 %collective-permute-start.16 = (bf16[128,4096]{1,0:T(8,128)(2,1)S(1)}, bf16[128,4096]{1,0:T(8,128)(2,1)S(1)}, u32[]{:S(2)}, u32[]{:S(2)}) collective-permute-start(bf16[128,4096]{1,0:T(8,128)(2,1)S(1)} %constant_dynamic-update-slice_fusion.2.near_ref), channel_id=1, source_target_pairs={{0,8},{1,9},{2,10},{3,11},{4,12},{5,13},{6,14},{7,15},{8,0},{9,1},... | collective-permute-start | bytes 3145736 | tf_op jit(solution)/shard_map/ppermute | solution.py:25
  47.0 5.2 %collective-permute-start.15 = (f32[64,128]{1,0:T(8,128)S(1)}, f32[64,128]{1,0:T(8,128)S(1)}, u32[]{:S(2)}, u32[]{:S(2)}) collective-permute-start(f32[64,128]{1,0:T(8,128)S(1)} %add.20), channel_id=1, source_target_pairs={{0,48},{1,49},{2,50},{3,51},{4,52},{5,53},{6,54},{7,55},{8,56},{9,... | collective-permute-start | bytes 98312 | tf_op jit(solution)/shard_map/ppermute | solution.py:25
  49.1 5.7 %collective-permute-start.14 = (f32[64,128]{1,0:T(8,128)S(1)}, f32[64,128]{1,0:T(8,128)S(1)}, u32[]{:S(2)}, u32[]{:S(2)}) collective-permute-start(f32[64,128]{1,0:T(8,128)S(1)} %add.20), channel_id=1, source_target_pairs={{0,32},{1,33},{2,34},{3,35},{4,36},{5,37},{6,38},{7,39},{8,40},{9,... | collective-permute-start | bytes 98312 | tf_op jit(solution)/shard_map/ppermute | solution.py:25
  50.1 4.8 %collective-permute-start.13 = (f32[64,128]{1,0:T(8,128)S(1)}, f32[64,128]{1,0:T(8,128)S(1)}, u32[]{:S(2)}, u32[]{:S(2)}) collective-permute-start(f32[64,128]{1,0:T(8,128)S(1)} %add.20), channel_id=1, source_target_pairs={{0,16},{1,17},{2,18},{3,19},{4,20},{5,21},{6,22},{7,23},{8,24},{9,... | collective-permute-start | bytes 98312 | tf_op jit(solution)/shard_map/ppermute | solution.py:25
